TPU v7x, 32 devices: a whole 2x2x4 slice. The times are simulated.
32 devices in a mesh: dp: 16 (over z, y, x), seq: 2 (over core).
Axes of the slice: x: 2, y: 2, z: 4, core: 2. Of those that a mesh axis runs over, the one named last changes fastest.
Arguments:
- inputs: bfloat16 [64, 512, 1024], P('dp', 'seq'), may hold values from -6 to 6
- memory: bfloat16 [64, 512, 1024], P('dp', 'seq'), may hold values from -6 to 6
- compressed: bfloat16 [64, 512, 1024], P('dp', 'seq'), may hold values from -6 to 6
- offsets: int32 [64], P('dp'), may hold values from 0 to 1024, as said below
- resets: int32 [64], P('dp'), may hold values from 0 to 1, as said below
- w_query: bfloat16 [1024, 1024], replicated, may hold values from -0.1875 to 0.1875
- w_key: bfloat16 [1024, 1024], replicated, may hold values from -0.1875 to 0.1875
- w_value: bfloat16 [1024, 1024], replicated, may hold values from -0.1875 to 0.1875
- w_output: bfloat16 [1024, 1024], replicated, may hold values from -3 to 3
- w_hidden: bfloat16 [1024, 4096], P(None, 'seq'), may hold values from -0.1875 to 0.1875
- w_return: bfloat16 [4096, 1024], P('seq'), may hold values from -0.09375 to 0.09375
- w_compress: bfloat16 [3072, 1024], replicated, may hold values from -0.109375 to 0.109375
- gain_attn: bfloat16 [1024], replicated, may hold values from 0.099609375 to 1.8984375
- gain_ffn: bfloat16 [1024], replicated, may hold values from 0.099609375 to 1.8984375
- out_grad: bfloat16 [64, 512, 1024], P('dp', 'seq'), may hold values from -6 to 6
- comp_grad: bfloat16 [64, 170, 1024], P('dp'), may hold values from -6 to 6
Outputs:
- outputs: bfloat16 [64, 512, 1024], P('dp', 'seq')
- new_compressed: bfloat16 [64, 170, 1024], P('dp')
- input_grad: bfloat16 [64, 512, 1024], P('dp', 'seq')
- grad_query: float32 [1024, 1024], P('dp', 'seq')
- grad_key: float32 [1024, 1024], P('dp', 'seq')
- grad_value: float32 [1024, 1024], P('dp', 'seq')
- grad_output: float32 [1024, 1024], P('dp', 'seq')
- grad_hidden: float32 [1024, 4096], P('dp', 'seq')
- grad_return: float32 [4096, 1024], P('seq', 'dp')
- grad_compress: float32 [3072, 1024], P('dp', 'seq')
- grad_gain_attn: float32 [1024], P('dp')
- grad_gain_ffn: float32 [1024], P('dp')
Inputs may be any that keep to these rules, and one draw needn't show every extreme that they name: `offsets`: memory slots count oldest first, the 512 compressed slots before the 512 memory slots; slots below a stream's offset are masked. In each block of 4 consecutive streams one stream, at a place drawn from the seed, has offset 0 and reset 0, and the next stream of the block (cyclically) has offset 2 * 512. `resets`: A 1 clears the stream's memories: all its memory slots are masked and its memory enters the compression as zeros. In each block of 4 consecutive streams the stream two places after the one with offset 0 (cyclically) has reset 1.
All inputs are finite; a program needn't handle non-finite values.
Results may differ from a plain program's by a relative error of at most 0.018.
Values may be sent and summed in bfloat16 or wider, within the bound.
A program may use at most 384 MiB of HBM per device.

v0:
```python
import jax
import jax.numpy as jnp
from jax import lax
from jax.sharding import PartitionSpec as P

HEADS = 8
HEAD_DIM = 128
RATE = 3


epsilon = 1e-05
masked_score = -1e30


def shifted(block, axis, distance):
    devices = range(lax.axis_size(axis))
    route = [(i - distance, i) for i in devices if i - distance in devices]
    return lax.ppermute(block, axis, route)


def layer_norm(values, gain):
    centred = values - jnp.mean(values, axis=-1, keepdims=True)
    spread = jnp.mean(centred * centred, axis=-1, keepdims=True)
    return centred * lax.rsqrt(spread + epsilon) * gain


def project(left, right):
    return jnp.einsum("srd,de->sre", left, right, preferred_element_type=jnp.float32)


def project_back(left, right):
    return jnp.einsum("sre,de->srd", left, right, preferred_element_type=jnp.float32)


def weight_term(left, right):
    return jnp.einsum("srd,sre->de", left, right, preferred_element_type=jnp.float32)


def key_layout(key_index, local_rows, seg_len):
    key_owner = key_index // (3 * local_rows)
    inside = key_index % (3 * local_rows)
    key_kind = inside // local_rows
    key_place = key_owner * local_rows + inside % local_rows
    mem_slot = jnp.where(key_kind == 0, key_place, seg_len + key_place)
    return (key_kind, mem_slot, key_place)


def allowed_mask(key_kind, mem_slot, key_place, query_place, offsets, keep_flag):
    memory_ok = (mem_slot[None, :] >= offsets[:, None]) & keep_flag[:, None]
    causal = key_place[None, :] <= query_place[:, None]
    return jnp.where(key_kind[None, None, :] < 2, memory_ok[:, None, :], causal[None, :, :])


def score_block(query_heads, key_heads, allowed, score_scale):
    scores = (
        jnp.einsum("sthe,skhe->shtk", query_heads, key_heads, preferred_element_type=jnp.float32)
        * score_scale
    )
    return jnp.where(allowed[:, None], scores, masked_score)


def tile_matrix(matrix, dp_count, seq_count):
    rows_total, cols_total = matrix.shape
    blocks = matrix.reshape(dp_count, rows_total // dp_count, seq_count, cols_total // seq_count)
    return blocks.transpose(0, 2, 1, 3).reshape(
        dp_count * seq_count, rows_total // dp_count, cols_total // seq_count
    )


def tile_vector(vector, dp_count, seq_count):
    piece_len = vector.shape[0] // dp_count
    pieces = vector.reshape(dp_count, 1, piece_len)
    return jnp.broadcast_to(pieces, (dp_count, seq_count, piece_len)).reshape(
        dp_count * seq_count, piece_len
    )


def on_device(
    inputs,
    memory,
    compressed,
    offsets,
    resets,
    w_query,
    w_key,
    w_value,
    w_output,
    w_hidden,
    w_return,
    w_compress,
    gain_attn,
    gain_ffn,
    out_grad,
    comp_grad,
):
    seq_count = lax.axis_size("seq")
    dp_count = lax.axis_size("dp")
    seq_rank = lax.axis_index("seq")
    streams, local_rows, feat_width = inputs.shape
    seg_len = local_rows * seq_count
    score_scale = HEAD_DIM ** (-0.5)
    keep_flag = resets == 0
    all_rows = jnp.concatenate([compressed, memory, inputs], axis=1).astype(jnp.float32)
    normed, attn_norm_back = jax.vjp(layer_norm, all_rows, gain_attn.astype(jnp.float32))
    normed_low = normed.astype(jnp.bfloat16)
    query_in = normed_low[:, 2 * local_rows :]
    query_low = project(query_in, w_query).astype(jnp.bfloat16)
    key_low = project(normed_low, w_key).astype(jnp.bfloat16)
    value_low = project(normed_low, w_value).astype(jnp.bfloat16)
    key_all, value_all = (
        lax.all_gather(key_low, "seq", axis=1, tiled=True),
        lax.all_gather(value_low, "seq", axis=1, tiled=True),
    )
    total_keys = key_all.shape[1]
    key_kind, mem_slot, key_place = key_layout(
        jnp.arange(total_keys, dtype=jnp.int32), local_rows, seg_len
    )
    query_place = seq_rank * local_rows + jnp.arange(local_rows, dtype=jnp.int32)
    allowed = allowed_mask(key_kind, mem_slot, key_place, query_place, offsets, keep_flag)
    query_heads = query_low.reshape(streams, local_rows, HEADS, HEAD_DIM)
    key_heads = key_all.reshape(streams, total_keys, HEADS, HEAD_DIM)
    value_heads = value_all.reshape(streams, total_keys, HEADS, HEAD_DIM)
    scores = score_block(query_heads, key_heads, allowed, score_scale)
    row_top = jnp.max(scores, axis=-1, keepdims=True)
    exp_scores = jnp.exp(scores - row_top)
    row_total = jnp.sum(exp_scores, axis=-1, keepdims=True)
    attn_prob = exp_scores / row_total
    log_total = row_top + jnp.log(row_total)
    mixed_low = (
        jnp.einsum(
            "shtk,skhe->sthe",
            attn_prob.astype(jnp.bfloat16),
            value_heads,
            preferred_element_type=jnp.float32,
        )
        .reshape(streams, local_rows, feat_width)
        .astype(jnp.bfloat16)
    )
    hidden = inputs.astype(jnp.float32) + project(mixed_low, w_output)
    ffn_in, ffn_norm_back = jax.vjp(layer_norm, hidden, gain_ffn.astype(jnp.float32))
    ffn_low = ffn_in.astype(jnp.bfloat16)
    ffn_all = lax.all_gather(ffn_low, "seq", axis=1, tiled=True)
    pre_act = jnp.einsum("std,df->stf", ffn_all, w_hidden, preferred_element_type=jnp.float32)
    act_float, gelu_back = jax.vjp(jax.nn.gelu, pre_act)
    act_low = act_float.astype(jnp.bfloat16)
    partial_out = jnp.einsum("stf,fd->std", act_low, w_return, preferred_element_type=jnp.float32)
    ffn_out = lax.psum_scatter(
        partial_out.astype(jnp.bfloat16), "seq", scatter_dimension=1, tiled=True
    ).astype(jnp.float32)
    cot_all = lax.all_gather(out_grad, "seq", axis=1, tiled=True)
    act_grad = jnp.einsum("std,fd->stf", cot_all, w_return, preferred_element_type=jnp.float32)
    return_part = jnp.einsum("stf,std->fd", act_low, cot_all, preferred_element_type=jnp.float32)
    pre_grad = gelu_back(act_grad)[0].astype(jnp.bfloat16)
    hidden_part = jnp.einsum("std,stf->df", ffn_all, pre_grad, preferred_element_type=jnp.float32)
    in_part = jnp.einsum("stf,df->std", pre_grad, w_hidden, preferred_element_type=jnp.float32)
    ffn_in_grad = lax.psum_scatter(in_part, "seq", scatter_dimension=1, tiled=True)
    hidden_sum, return_sum = (
        lax.psum_scatter(
            hidden_part.astype(jnp.bfloat16), "dp", scatter_dimension=0, tiled=True
        ).astype(jnp.float32),
        lax.psum_scatter(
            return_part.T.astype(jnp.bfloat16), "dp", scatter_dimension=0, tiled=True
        ).astype(jnp.float32),
    )
    grad_return = return_sum.T
    outputs = (hidden + ffn_out).astype(jnp.bfloat16)
    hidden_grad, gain_ffn_grad = ffn_norm_back(ffn_in_grad)
    hidden_grad = hidden_grad + out_grad.astype(jnp.float32)
    attn_grad_low = hidden_grad.astype(jnp.bfloat16)
    output_part = weight_term(mixed_low, attn_grad_low)
    mixed_grad = project_back(attn_grad_low, w_output).astype(jnp.bfloat16)
    mixed_heads = mixed_grad.reshape(streams, local_rows, HEADS, HEAD_DIM)
    prob_again = jnp.exp(score_block(query_heads, key_heads, allowed, score_scale) - log_total)
    prob_grad = jnp.einsum(
        "sthe,skhe->shtk", mixed_heads, value_heads, preferred_element_type=jnp.float32
    )
    prob_delta = jnp.sum(prob_again * prob_grad, axis=-1)
    score_grad = (prob_again * (prob_grad - prob_delta[..., None])).astype(jnp.bfloat16)
    query_grad = (
        (
            jnp.einsum("shtk,skhe->sthe", score_grad, key_heads, preferred_element_type=jnp.float32)
            * score_scale
        )
        .reshape(streams, local_rows, feat_width)
        .astype(jnp.bfloat16)
    )
    key_part = (
        jnp.einsum("shtk,sthe->skhe", score_grad, query_heads, preferred_element_type=jnp.float32)
        * score_scale
    ).reshape(streams, total_keys, feat_width)
    value_part = jnp.einsum(
        "shtk,sthe->skhe",
        prob_again.astype(jnp.bfloat16),
        mixed_heads,
        preferred_element_type=jnp.float32,
    ).reshape(streams, total_keys, feat_width)
    key_sum, value_sum = (
        lax.psum_scatter(
            key_part.astype(jnp.bfloat16), "seq", scatter_dimension=1, tiled=True
        ).astype(jnp.float32),
        lax.psum_scatter(
            value_part.astype(jnp.bfloat16), "seq", scatter_dimension=1, tiled=True
        ).astype(jnp.float32),
    )
    key_grad = key_sum.astype(jnp.bfloat16)
    value_grad = value_sum.astype(jnp.bfloat16)
    query_part = weight_term(query_in, query_grad)
    key_wpart = weight_term(normed_low, key_grad)
    value_wpart = weight_term(normed_low, value_grad)
    query_back = project_back(query_grad, w_query)
    normed_grad = project_back(key_grad, w_key) + project_back(value_grad, w_value)
    normed_grad = normed_grad + jnp.concatenate(
        [jnp.zeros((streams, 2 * local_rows, feat_width), jnp.float32), query_back], axis=1
    )
    rows_grad, gain_attn_grad = attn_norm_back(normed_grad)
    input_grad = (rows_grad[:, 2 * local_rows :] + hidden_grad).astype(jnp.bfloat16)
    kept_memory = memory * keep_flag[:, None, None].astype(jnp.bfloat16)
    edge_rows = shifted(kept_memory[:, : 2 * (RATE - 1)], "seq", -1)
    extended = jnp.concatenate([kept_memory, edge_rows], axis=1)
    group_count = (local_rows + RATE - 1) // RATE
    first_group = (seq_rank * local_rows + RATE - 1) // RATE
    slice_start = RATE * first_group - seq_rank * local_rows
    grouped = lax.dynamic_slice_in_dim(extended, slice_start, RATE * group_count, 1).reshape(
        streams, group_count, RATE * feat_width
    )
    piece_rows = jnp.einsum(
        "sgc,cd->sgd", grouped, w_compress, preferred_element_type=jnp.float32
    ).astype(jnp.bfloat16)
    comp_all = lax.all_gather(piece_rows, "seq", axis=1, tiled=True)
    comp_count = comp_grad.shape[1]
    out_index = jnp.arange(comp_count, dtype=jnp.int32)
    holder = RATE * out_index // local_rows
    lookup = holder * group_count + out_index - (holder * local_rows + RATE - 1) // RATE
    new_compressed = jnp.take(comp_all, lookup, axis=1)
    slot_index = first_group + jnp.arange(group_count, dtype=jnp.int32)
    slot_valid = (RATE * slot_index < (seq_rank + 1) * local_rows) & (slot_index < comp_count)
    picked = jnp.take(comp_grad, jnp.minimum(slot_index, comp_count - 1), axis=1) * slot_valid[
        None, :, None
    ].astype(jnp.bfloat16)
    compress_part = jnp.einsum("sgc,sgd->cd", grouped, picked, preferred_element_type=jnp.float32)
    reduced = (
        lax.psum_scatter(
            tile_matrix(query_part, dp_count, seq_count),
            ("dp", "seq"),
            scatter_dimension=0,
            tiled=True,
        ),
        lax.psum_scatter(
            tile_matrix(key_wpart, dp_count, seq_count),
            ("dp", "seq"),
            scatter_dimension=0,
            tiled=True,
        ),
        lax.psum_scatter(
            tile_matrix(value_wpart, dp_count, seq_count),
            ("dp", "seq"),
            scatter_dimension=0,
            tiled=True,
        ),
        lax.psum_scatter(
            tile_matrix(output_part, dp_count, seq_count),
            ("dp", "seq"),
            scatter_dimension=0,
            tiled=True,
        ),
        lax.psum_scatter(
            tile_matrix(compress_part, dp_count, seq_count),
            ("dp", "seq"),
            scatter_dimension=0,
            tiled=True,
        ),
        lax.psum_scatter(
            tile_vector(gain_attn_grad, dp_count, seq_count),
            ("dp", "seq"),
            scatter_dimension=0,
            tiled=True,
        ),
        lax.psum_scatter(
            tile_vector(gain_ffn_grad, dp_count, seq_count),
            ("dp", "seq"),
            scatter_dimension=0,
            tiled=True,
        ),
    )
    return (
        outputs,
        new_compressed,
        input_grad,
        reduced[0][0],
        reduced[1][0],
        reduced[2][0],
        reduced[3][0],
        hidden_sum,
        grad_return,
        reduced[4][0],
        reduced[5][0],
        reduced[6][0],
    )


def solution(mesh):
    placed = (
        P("dp", "seq", None),
        P("dp", "seq", None),
        P("dp", "seq", None),
        P("dp"),
        P("dp"),
        P(),
        P(),
        P(),
        P(),
        P(None, "seq"),
        P("seq", None),
        P(),
        P(),
        P(),
        P("dp", "seq", None),
        P("dp", None, None),
    )
    return jax.shard_map(
        on_device,
        mesh=mesh,
        in_specs=placed,
        out_specs=(
            P("dp", "seq", None),
            P("dp", None, None),
            P("dp", "seq", None),
            P("dp", "seq"),
            P("dp", "seq"),
            P("dp", "seq"),
            P("dp", "seq"),
            P("dp", "seq"),
            P("seq", "dp"),
            P("dp", "seq"),
            P("dp"),
            P("dp"),
        ),
        check_vma=False,
    )
```

profile of v0, /device:TPU:0, one launch (start us, length us, event | category | flops | bytes accessed | tf_op | source)
XLA Modules:
  0.0 1407.0 jit_solution(1692295044814560454)
XLA Ops:
  32.9 11.9 convolution_convert_fusion.1
  60.1 17.1 %copy.127 = bf16[4,1536,1024]{1,2,0:T(8,128)(2,1)} copy(bf16[4,1536,1024]{2,1,0:T(8,128)(2,1)} %all-gather.8.cloned.1.call-done) | data formatting | bytes 25165824 | tf_op jit(solution)/shard_map/reshape | solution.py:121
  77.2 25.5 %fusion.109 = (f32[4,8,256]{2,1,0:T(8,128)S(1)}, f32[4,8,256,1536]{3,2,1,0:T(8,128)}) fusion(bf16[4,256,8,128]{1,3,2,0:T(8,128)(2,1)} %bitcast.198, bf16[4,1536,8,128]{1,3,2,0:T(8,128)(2,1)} %bitcast.192, pred[4,256,1536]{2,1,0:T(8,128)(4,1)} %broadcast_select_fusion), kind=kOutput, calls=%fused_computation.186 | convolution fusion | flops 3258966016 | bytes 66617344 | tf_op jit(solution)/shard_map/sthe,skhe->shtk/dot_general | solution.py:56
  102.7 21.1 %fusion = f32[4,8,256]{2,1,0:T(8,128)S(1)} fusion(f32[4,8,256,1536]{3,2,1,0:T(8,128)} %get-tuple-element.62, f32[4,8,256]{2,1,0:T(8,128)S(1)} %get-tuple-element.61), kind=kLoop, calls=%fused_computation.8 | loop fusion | flops 25157632 | bytes 50397184 | tf_op jit(solution)/shard_map/reduce_sum | solution.py:126
  123.8 23.7 %fusion.71 = bf16[4,8,128,256]{3,2,1,0:T(8,128)(2,1)} fusion(f32[4,8,256,1536]{3,2,1,0:T(8,128)} %get-tuple-element.62, f32[4,8,256]{2,1,0:T(8,128)S(1)} %fusion, f32[4,8,256]{2,1,0:T(8,128)S(1)} %get-tuple-element.61, bf16[4,1536,1024]{2,1,0:T(8,128)(2,1)} %all-gather.6.cloned.1.call-done), kind=kOutput, calls=%fused_computation.99 | convolution fusion | flops 3260022784 | bytes 65077248 | tf_op jit(solution)/shard_map/shtk,skhe->sthe/dot_general | solution.py:130
  157.5 14.9 %all-gather.10.cloned.1.call-done = bf16[4,512,1024]{2,1,0:T(8,128)(2,1)} async-done(((bf16[4,256,1024]{2,1,0:T(8,128)(2,1)}), bf16[4,512,1024]{2,1,0:T(8,128)(2,1)}) %all-gather.10.cloned.1.call-update) | async-done | bytes 4194320 | tf_op jit(solution)/shard_map/all_gather | solution.py:142
  172.4 15.4 %fusion.40 = f32[4,512,2048]{2,1,0:T(8,128)} fusion(bf16[4,512,1024]{2,1,0:T(8,128)(2,1)} %all-gather.10.cloned.1.call-done, bf16[1024,2048]{1,0:T(8,128)(2,1)} %param.25), kind=kOutput, calls=%fused_computation.58 | convolution fusion | flops 8589934592 | bytes 25165824 | tf_op jit(solution)/shard_map/std,df->stf/dot_general | solution.py:143
  188.7 26.2 %fusion.12 = bf16[4,512,2048]{2,1,0:T(8,128)(2,1)} fusion(f32[4,512,2048]{2,1,0:T(8,128)} %fusion.40, bf16[4,512,1024]{2,1,0:T(8,128)(2,1)} %all-gather.14.cloned.1.call-done, bf16[2048,1024]{1,0:T(8,128)(2,1)} %param.26), kind=kOutput, calls=%fused_computation.23 | convolution fusion | flops 8673820672 | bytes 33554432 | tf_op jit(solution)/shard_map/std,fd->stf/dot_general | solution.py:151
  214.9 13.9 fusion.38
  228.9 16.1 %fusion.45 = bf16[4,512,1024]{2,1,0:T(8,128)(2,1)} fusion(bf16[2048,1024]{1,0:T(8,128)(2,1)} %param.26, f32[4,512,2048]{2,1,0:T(8,128)} %fusion.40), kind=kOutput, calls=%fused_computation.74 | convolution fusion | flops 8629780480 | bytes 25165824 | tf_op jit(solution)/shard_map/stf,fd->std/dot_general | solution.py:146
  251.9 10.7 reduce-scatter.14.cloned.1.call-done
  280.2 22.6 %fusion.19 = bf16[4,8,128,1536]{3,2,1,0:T(8,128)(2,1)} fusion(bf16[4,256,8,128]{1,3,2,0:T(8,128)(2,1)} %bitcast.196, f32[4,8,256,1536]{3,2,1,0:T(8,128)} %get-tuple-element.62, f32[4,8,256]{2,1,0:T(8,128)S(1)} %log_add_fusion), kind=kOutput, calls=%fused_computation.33 | convolution fusion | flops 3252682752 | bytes 65044480 | tf_op jit(solution)/shard_map/shtk,sthe->skhe/dot_general | solution.py:191
  302.8 16.7 %copy.89 = bf16[4,1536,1024]{2,1,0:T(8,128)(2,1)} copy(bf16[4,1536,1024]{1,2,0:T(8,128)(2,1)} %bitcast.195) | data formatting | bytes 25165824 | tf_op jit(solution)/shard_map/convert_element_type | solution.py:202
  319.5 41.7 %multiply_reduce_fusion = (f32[4,8,256]{2,1,0:T(8,128)S(1)}, f32[4,8,256,1536]{3,2,1,0:T(8,128)}) fusion(f32[4,8,256,1536]{3,2,1,0:T(8,128)} %get-tuple-element.62, f32[4,8,256]{2,1,0:T(8,128)S(1)} %log_add_fusion, bf16[4,256,8,128]{1,3,2,0:T(8,128)(2,1)} %bitcast.197, bf16[4,1536,1024]{2,1,0:T(8,128)(2,1)} %all-gather.6.cloned.1.call-done), kind=kOutput, calls=%fused_computation.3 | convolution fusion | flops 3258966016 | bytes 115408896 | tf_op jit(solution)/shard_map/sthe,skhe->shtk/dot_general | solution.py:174
  361.2 40.8 %multiply_convert_fusion = bf16[4,8,256,1536]{3,2,1,0:T(8,128)(2,1)} fusion(f32[4,8,256,1536]{3,2,1,0:T(8,128)} %get-tuple-element.66, f32[4,8,256,1536]{3,2,1,0:T(8,128)} %get-tuple-element.62, f32[4,8,256]{2,1,0:T(8,128)S(1)} %get-tuple-element.65, f32[4,8,256]{2,1,0:T(8,128)S(1)} %log_add_fusion), kind=kLoop, calls=%fused_computation.2 | loop fusion | flops 50331648 | bytes 125894656 | tf_op jit(solution)/shard_map/convert_element_type | solution.py:178
  402.0 15.0 %multiply_convert_fusion.1 = bf16[4,8,128,1536]{3,2,1,0:T(8,128)(2,1)} fusion(bf16[4,256,8,128]{1,3,2,0:T(8,128)(2,1)} %bitcast.199, bf16[4,8,256,1536]{3,2,1,0:T(8,128)(2,1)} %multiply_convert_fusion), kind=kOutput, calls=%fused_computation.11 | convolution fusion | flops 3233808384 | bytes 39845888 | tf_op jit(solution)/shard_map/shtk,sthe->skhe/dot_general | solution.py:188
  417.0 16.6 %copy.87 = bf16[4,1536,1024]{2,1,0:T(8,128)(2,1)} copy(bf16[4,1536,1024]{1,2,0:T(8,128)(2,1)} %bitcast.194) | data formatting | bytes 25165824 | tf_op jit(solution)/shard_map/convert_element_type | solution.py:199
  458.8 17.4 %fusion.42 = bf16[1024,2048]{0,1:T(8,128)(2,1)} fusion(bf16[4,512,1024]{2,1,0:T(8,128)(2,1)} %all-gather.14.cloned.1.call-done, f32[4,512,2048]{2,1,0:T(8,128)} %fusion.40), kind=kOutput, calls=%fused_computation.70 | convolution fusion | flops 8629780480 | bytes 25165824 | tf_op jit(solution)/shard_map/stf,std->fd/dot_general | solution.py:152
  482.7 14.1 bitcast_convert_fusion.1
  506.1 9.3 fusion.43
  539.9 15.7 %multiply_convert_fusion.3 = bf16[4,8,128,256]{3,2,1,0:T(8,128)(2,1)S(1)} fusion(bf16[4,1536,8,128]{1,3,2,0:T(8,128)(2,1)} %bitcast.193, bf16[4,8,256,1536]{3,2,1,0:T(8,128)(2,1)} %multiply_convert_fusion), kind=kOutput, calls=%fused_computation.61 | convolution fusion | flops 3223322624 | bytes 39845888 | tf_op jit(solution)/shard_map/shtk,skhe->sthe/dot_general | solution.py:181
  560.2 12.1 convolution_bitcast_fusion
  584.0 12.4 convolution_bitcast_fusion.1
  617.2 58.9 %reduce-scatter.30.cloned.1.call-done = bf16[64,2048]{1,0:T(8,128)(2,1)} async-done(((bf16[1024,2048]{1,0:T(8,128)(2,1)}), bf16[64,2048]{1,0:T(8,128)(2,1)}) %reduce-scatter.30.cloned.1.call-update) | async-done | bytes 262160 | tf_op jit(solution)/shard_map/reduce_scatter | solution.py:158
  685.3 13.1 fusion.59
  698.4 16.9 %fusion.23 = (f32[1024]{0:T(1024)}, f32[4,768]{1,0:T(4,128)}, f32[4,768,1024]{2,1,0:T(8,128)S(1)}) fusion(f32[4,768]{1,0:T(4,128)S(1)} %copy-done.18, f32[4,768]{1,0:T(4,128)S(1)} %copy-done.16, bf16[4,256,1024]{2,1,0:T(8,128)(2,1)S(1)} %copy-done.6, bf16[4,256,1024]{2,1,0:T(8,128)(2,1)S(1)} %copy-done.3, bf16[4,256,1024]{2,1,0:T(8,128)(2,1)S(1)} %copy-done.8, ...), kind=kOutput, calls=%fused_computation.35 | convolution fusion | flops 6489632768 | bytes 44085248 | tf_op jit(solution)/shard_map/sre,de->srd/dot_general | solution.py:32
  723.2 40.7 %all-reduce.3 = (f32[32,64]{1,0:T(8,128)S(1)}, f32[32,64]{1,0:T(8,128)S(1)}) all-reduce(f32[32,64]{1,0:T(8,128)S(1)} %bitcast.214, f32[32,64]{1,0:T(8,128)S(1)} %bitcast.213), channel_id=13, replica_groups=mesh['dp'=16,'seq'=2] {'dp','seq'}, use_global_device_ids=true, to_apply=%region_23.24.clone | all-reduce | flops 4096 | bytes 32768
  770.3 68.1 %reduce-scatter.32.cloned.1.call-done = f32[1,192,512]{2,1,0:T(8,128)} async-done(((f32[32,192,512]{2,1,0:T(8,128)}), f32[1,192,512]{2,1,0:T(8,128)}) %reduce-scatter.32.cloned.1.call-update) | async-done | bytes 393232 | tf_op jit(solution)/shard_map/reduce_scatter | solution.py:266
  838.3 143.0 %reduce-scatter.28.cloned.1.call-done = f32[1,64,512]{2,1,0:T(8,128)} async-done(((f32[32,64,512]{2,1,0:T(8,128)}), f32[1,64,512]{2,1,0:T(8,128)}) %reduce-scatter.28.cloned.1.call-update) | async-done | bytes 131088 | tf_op jit(solution)/shard_map/reduce_scatter | solution.py:260
  981.3 139.6 %reduce-scatter.22.cloned.1.call-done = f32[1,64,512]{2,1,0:T(8,128)} async-done(((f32[32,64,512]{2,1,0:T(8,128)}), f32[1,64,512]{2,1,0:T(8,128)}) %reduce-scatter.22.cloned.1.call-update) | async-done | bytes 131088 | tf_op jit(solution)/shard_map/reduce_scatter | solution.py:242
  1120.9 139.6 %reduce-scatter.26.cloned.1.call-done = f32[1,64,512]{2,1,0:T(8,128)} async-done(((f32[32,64,512]{2,1,0:T(8,128)}), f32[1,64,512]{2,1,0:T(8,128)}) %reduce-scatter.26.cloned.1.call-update) | async-done | bytes 131088 | tf_op jit(solution)/shard_map/reduce_scatter | solution.py:254
  1260.5 139.6 %reduce-scatter.24.cloned.1.call-done = f32[1,64,512]{2,1,0:T(8,128)} async-done(((f32[32,64,512]{2,1,0:T(8,128)}), f32[1,64,512]{2,1,0:T(8,128)}) %reduce-scatter.24.cloned.1.call-update) | async-done | bytes 131088 | tf_op jit(solution)/shard_map/reduce_scatter | solution.py:248
  (187 shorter events, 201.9 us)
Async XLA Ops:
  7.2 25.7 %copy-start = (bf16[1024,1024]{1,0:T(8,128)(2,1)S(1)}, bf16[1024,1024]{1,0:T(8,128)(2,1)}, u32[]{:S(2)}) copy-start(bf16[1024,1024]{1,0:T(8,128)(2,1)} %param.23) | copy-start | bytes 6291460
  7.2 52.9 %all-gather.8.cloned.1.call-start = ((), (), s32[]{:S(2)}) async-start(), calls=%async_computation.12 | async-start | bytes 18874368 | tf_op jit(solution)/shard_map/all_gather | solution.py:111
  8.1 10.6 copy-start.21
  32.8 91.0 %all-gather.6.cloned.1.call-start = ((), (), s32[]{:S(2)}) async-start(), calls=%async_computation.11 | async-start | bytes 18874368 | tf_op jit(solution)/shard_map/all_gather | solution.py:112
  44.8 127.7 %all-gather.10.cloned.1.call-start = ((), (), s32[]{:S(2)}) async-start(), calls=%async_computation.13 | async-start | bytes 6291456 | tf_op jit(solution)/shard_map/all_gather | solution.py:142
  45.4 11.1 copy-start.34
  45.4 11.6 copy-start.29
  156.9 31.8 %all-gather.14.cloned.1.call-start = ((), (), s32[]{:S(2)}) async-start(), calls=%async_computation.16 | async-start | bytes 6291456 | tf_op jit(solution)/shard_map/all_gather | solution.py:150
  157.5 89.5 %reduce-scatter.16.cloned.1.call-start = ((), (), s32[]{:S(2)}) async-start(), calls=%async_computation.17 | async-start | bytes 12582912 | tf_op jit(solution)/shard_map/reduce_scatter | solution.py:156
  188.7 26.2 %copy-start.30 = (bf16[1024,2048]{1,0:T(8,128)(2,1)S(1)}, bf16[1024,2048]{1,0:T(8,128)(2,1)}, u32[]{:S(2)}) copy-start(bf16[1024,2048]{1,0:T(8,128)(2,1)} %param.25) | copy-start | bytes 12582916
  228.8 33.7 %reduce-scatter.14.cloned.1.call-start = ((), (), s32[]{:S(2)}) async-start(), calls=%async_computation.14 | async-start | bytes 6291456 | tf_op jit(solution)/shard_map/reduce_scatter | solution.py:147
  245.0 315.1 %reduce-scatter.20.cloned.1.call-start = ((), (), s32[]{:S(2)}) async-start(), calls=%async_computation.19 | async-start | bytes 18874368 | tf_op jit(solution)/shard_map/reduce_scatter | solution.py:201
  319.5 264.5 %reduce-scatter.18.cloned.1.call-start = ((), (), s32[]{:S(2)}) async-start(), calls=%async_computation.18 | async-start | bytes 18874368 | tf_op jit(solution)/shard_map/reduce_scatter | solution.py:198
  433.6 174.4 %all-gather.12.cloned.1.call-start = ((), (), s32[]{:S(2)}) async-start(), calls=%async_computation.15 | async-start | bytes 2113536 | tf_op jit(solution)/shard_map/all_gather | solution.py:229
  437.4 3.1 collective-permute-start
  458.7 154.3 %reduce-scatter.34.cloned.1.call-start = ((), (), s32[]{:S(2)}) async-start(), calls=%async_computation.26 | async-start | bytes 4456448
  482.7 193.4 %reduce-scatter.30.cloned.1.call-start = ((), (), s32[]{:S(2)}) async-start(), calls=%async_computation.24 | async-start | bytes 4456448 | tf_op jit(solution)/shard_map/reduce_scatter | solution.py:158
  496.8 341.5 %reduce-scatter.32.cloned.1.call-start = ((), (), s32[]{:S(2)}) async-start(), calls=%async_computation.25 | async-start | bytes 12976128 | tf_op jit(solution)/shard_map/reduce_scatter | solution.py:266
  515.4 465.9 %reduce-scatter.28.cloned.1.call-start = ((), (), s32[]{:S(2)}) async-start(), calls=%async_computation.23 | async-start | bytes 4325376 | tf_op jit(solution)/shard_map/reduce_scatter | solution.py:260
  532.8 588.1 %reduce-scatter.22.cloned.1.call-start = ((), (), s32[]{:S(2)}) async-start(), calls=%async_computation.20 | async-start | bytes 4325376 | tf_op jit(solution)/shard_map/reduce_scatter | solution.py:242
  539.9 15.8 %copy-start.14 = (bf16[1024,256,4]{1,0,2:T(8,128)(2,1)S(1)}, bf16[1024,256,4]{1,0,2:T(8,128)(2,1)}, u32[]{:S(2)}) copy-start(bf16[1024,256,4]{1,0,2:T(8,128)(2,1)} %copy.92) | copy-start | bytes 6291460
  560.1 700.4 %reduce-scatter.26.cloned.1.call-start = ((), (), s32[]{:S(2)}) async-start(), calls=%async_computation.22 | async-start | bytes 4325376 | tf_op jit(solution)/shard_map/reduce_scatter | solution.py:254
  583.9 816.2 %reduce-scatter.24.cloned.1.call-start = ((), (), s32[]{:S(2)}) async-start(), calls=%async_computation.21 | async-start | bytes 4325376 | tf_op jit(solution)/shard_map/reduce_scatter | solution.py:248
  607.9 69.9 %copy-start.26 = (f32[1024]{0:T(1024)S(1)}, f32[1024]{0:T(1024)}, u32[]{:S(2)}) copy-start(f32[1024]{0:T(1024)} %get-tuple-element.50) | copy-start | bytes 12292
  685.2 13.1 copy-start.3
  685.2 13.1 copy-start.6
  685.2 13.1 copy-start.8
  685.3 13.1 copy-start.16
  685.3 13.1 copy-start.18
  685.3 13.1 copy-start.22
  698.4 16.9 %copy-start.20 = (f32[4,768]{1,0:T(4,128)S(1)}, f32[4,768]{1,0:T(4,128)}, u32[]{:S(2)}) copy-start(f32[4,768]{1,0:T(4,128)} %copy-done.19) | copy-start | bytes 36868
  716.1 48.4 %copy-start.24 = (f32[4,256]{1,0:T(4,128)S(1)}, f32[4,256]{1,0:T(4,128)}, u32[]{:S(2)}) copy-start(f32[4,256]{1,0:T(4,128)} %copy-done.23) | copy-start | bytes 12292
  (20 other events, 72.2 us)
Sparse Core Ops, SparseCore 0:
  32.9 27.1 all-gather.7
  61.6 25.5 all-gather.5
  157.0 15.3 all-gather.9
  173.8 14.8 all-gather.13
  228.9 17.9 reduce-scatter.15
  249.2 13.3 reduce-scatter.13
  319.6 22.7 reduce-scatter.19
  433.7 22.6 reduce-scatter.17
  458.8 10.6 all-gather.11
  482.8 96.2 reduce-scatter.33
  581.3 94.6 reduce-scatter.29
  682.5 155.7 reduce-scatter.31
  841.3 139.9 reduce-scatter.27
  984.1 136.7 reduce-scatter.21
  1123.7 136.7 reduce-scatter.25
  1263.3 136.7 reduce-scatter.23
where the time goes:
time: 1420 us; the launch traced here: 1410 us
  waiting for transfers between devices  720 us (51%)
  matrix products  373 us (26%)
  local copies, waits for them, and re-layouts  140 us (10%)
  other arithmetic  116 us (8%)
  blocking collectives  40.7 us (3%)
  between operations  15 us (1%)
    reduce_scatter x1, waiting for transfers between devices, on_device(): lax.psum_scatter(tile_matrix(output_part, dp_count, seq_count), ('dp', 's...  143 us
    reduce_scatter x1, waiting for transfers between devices, on_device(): lax.psum_scatter(tile_matrix(value_wpart, dp_count, seq_count), ('dp', 's...  140 us
    reduce_scatter x1, waiting for transfers between devices, on_device(): lax.psum_scatter(tile_matrix(query_part, dp_count, seq_count), ('dp', 'se...  140 us
    reduce_scatter x1, waiting for transfers between devices, on_device(): lax.psum_scatter(tile_matrix(key_wpart, dp_count, seq_count), ('dp', 'seq...  140 us
    reduce_scatter x1, waiting for transfers between devices, on_device(): lax.psum_scatter(tile_matrix(compress_part, dp_count, seq_count), ('dp',...  68.1 us
    reduce_scatter x1, waiting for transfers between devices, on_device(): lax.psum_scatter(hidden_part.astype(jnp.bfloat16), 'dp', scatter_dimensio...  58.9 us
    dot_general x1, matrix products, on_device(): jnp.einsum('sthe,skhe->shtk', mixed_heads, value_heads, preferred_element...  41.7 us
    convert_element_type x1, other arithmetic, on_device(): (prob_again * (prob_grad - prob_delta[..., None])).astype(jnp.bfloat16)  40.8 us
  transfers between devices with their start and end apart: 17, of which 12 were waited for; matrix products, arithmetic and copies ran while one was open for 33% of the time, Pallas kernels for 0%

commit v1 on v0

--- a/solution.py
+++ b/solution.py
@@ -1,6 +1,11 @@
+import functools
+import math
+
 import jax
 import jax.numpy as jnp
 from jax import lax
+from jax.experimental import pallas as pl
+from jax.experimental.pallas import tpu as pltpu
 from jax.sharding import PartitionSpec as P
 
 HEADS = 8
@@ -298,6 +303,607 @@
     )
 
 
+F32 = jnp.float32
+BF16 = jnp.bfloat16
+NN = (((1,), (0,)), ((), ()))
+NT = (((1,), (1,)), ((), ()))
+TN = (((0,), (0,)), ((), ()))
+VMEM_LIMIT = 60 * 1024 * 1024
+SCALE = HEAD_DIM ** (-0.5)
+EXP2_SCALE = SCALE * math.log2(math.e)
+
+
+def dot(left, right, dims=NN):
+    return lax.dot_general(left, right, dims, preferred_element_type=F32)
+
+
+def params(steps=1):
+    return pltpu.CompilerParams(
+        vmem_limit_bytes=VMEM_LIMIT, dimension_semantics=("arbitrary",) * steps
+    )
+
+
+def cost(flops, bytes_accessed=0, transcendentals=0):
+    return pl.CostEstimate(
+        flops=int(flops), bytes_accessed=int(bytes_accessed), transcendentals=int(transcendentals)
+    )
+
+
+def held(shape):
+    zeros = (0,) * len(shape)
+    return pl.BlockSpec(shape, lambda *_: zeros, pipeline_mode=pl.Buffered(1))
+
+
+def norm_parts(rows):
+    centred = rows - jnp.mean(rows, axis=-1, keepdims=True)
+    inverse = lax.rsqrt(jnp.mean(centred * centred, axis=-1, keepdims=True) + epsilon)
+    return centred * inverse, inverse
+
+
+def norm_back(grad, unit, inverse):
+    return inverse * (
+        grad
+        - jnp.mean(grad, axis=-1, keepdims=True)
+        - unit * jnp.mean(grad * unit, axis=-1, keepdims=True)
+    )
+
+
+def attn_fwd_kernel(
+    off_ref, q_ref, k_ref, v_ref, in_ref, wo_ref, gain_ref,
+    mixed_ref, hidden_ref, ffn_ref, lse_ref,
+):
+    step = pl.program_id(0)
+    half = q_ref.shape[0]
+    seg = 2 * half
+
+    def run(pieces):
+        def one_head(h, stats):
+            cols = pl.ds(pl.multiple_of(h * HEAD_DIM, HEAD_DIM), HEAD_DIM)
+            q = q_ref[:, cols]
+            scores = []
+            for start, size, kind in pieces:
+                s = dot(q, k_ref[start : start + size, cols], NT) * EXP2_SCALE
+                if kind == "mem":
+                    slot = lax.broadcasted_iota(jnp.int32, s.shape, 1)
+                    s = jnp.where(slot >= off_ref[0], s, masked_score)
+                if kind == "diag":
+                    key = lax.broadcasted_iota(jnp.int32, s.shape, 1)
+                    row = lax.broadcasted_iota(jnp.int32, s.shape, 0)
+                    s = jnp.where(key <= row, s, masked_score)
+                scores.append(s)
+            top = functools.reduce(
+                jnp.maximum, [jnp.max(s, axis=-1, keepdims=True) for s in scores]
+            )
+            total = jnp.zeros_like(top)
+            mix = jnp.zeros((half, HEAD_DIM), F32)
+            for s, (start, size, _) in zip(scores, pieces):
+                p = jnp.exp2(s - top)
+                total = total + jnp.sum(p, axis=-1, keepdims=True)
+                mix = mix + dot(p.astype(BF16), v_ref[start : start + size, cols])
+            mixed_ref[:, cols] = (mix / total).astype(BF16)
+            lane = lax.broadcasted_iota(jnp.int32, stats.shape, 1)
+            return jnp.where(lane == h, top + jnp.log2(total), stats)
+
+        stats = lax.fori_loop(0, HEADS, one_head, jnp.zeros((half, 128), F32))
+        lse_ref[...] = stats.T[:HEADS]
+
+    cases = (
+        ((0, 2 * seg, "mem"), (2 * seg, half, "diag")),
+        ((0, 2 * seg, "mem"), (2 * seg, half, "full"), (2 * seg + half, half, "diag")),
+        ((3 * seg, half, "diag"),),
+        ((3 * seg, half, "full"), (3 * seg + half, half, "diag")),
+    )
+    for i, pieces in enumerate(cases):
+        pl.when(step == i)(functools.partial(run, pieces))
+    hidden = in_ref[...].astype(F32) + dot(mixed_ref[...], wo_ref[...])
+    hidden_ref[...] = hidden
+    unit, _ = norm_parts(hidden)
+    ffn_ref[...] = (unit * gain_ref[...]).astype(BF16)
+
+
+def attn_fwd(first_slot, q, k, v, inputs, wo, gain):
+    rows, width = q.shape
+    half = rows // 4
+    by_block = pl.BlockSpec((half, width), lambda i: (i, 0))
+    return pl.pallas_call(
+        attn_fwd_kernel,
+        grid=(4,),
+        out_shape=(
+            jax.ShapeDtypeStruct((rows, width), BF16),
+            jax.ShapeDtypeStruct((rows, width), F32),
+            jax.ShapeDtypeStruct((rows, width), BF16),
+            jax.ShapeDtypeStruct((HEADS, rows), F32),
+        ),
+        in_specs=[
+            pl.BlockSpec(memory_space=pltpu.SMEM),
+            by_block, held(k.shape), held(v.shape), by_block, held(wo.shape), held(gain.shape),
+        ],
+        out_specs=(by_block, by_block, by_block, pl.BlockSpec((HEADS, half), lambda i: (0, i))),
+        compiler_params=params(),
+        cost_estimate=cost(20e9, 20e6),
+        name="attn_fwd",
+    )(first_slot, q, k, v, inputs, wo, gain)
+
+
+def attn_bwd_kernel(
+    off_ref, q_ref, k_ref, v_ref, do_ref, mixed_ref, lse_ref,
+    dq_ref, dk_ref, dv_ref,
+):
+    h = pl.program_id(0)
+    seg = q_ref.shape[0] // 2
+    half = seg // 2
+    for stream in range(2):
+        base = stream * seg
+        lse_row = lse_ref[pl.ds(h, 1), base : base + seg]
+        weight = do_ref[base : base + seg].astype(F32) * mixed_ref[base : base + seg].astype(F32)
+        delta_row = jnp.sum(weight.T, axis=0, keepdims=True)
+        key_base = 2 * seg + stream * seg
+        pieces = []
+        if stream == 0:
+            pieces += [(start, half, 0, "mem") for start in range(0, 2 * seg, half)]
+        pieces += [(key_base, half, 0, "diag"), (key_base + half, half, half, "diag")]
+        dq_low = jnp.zeros((half, HEAD_DIM), F32)
+        dq_high = jnp.zeros((half, HEAD_DIM), F32)
+        for start, size, first, kind in pieces:
+            q = q_ref[base + first : base + seg]
+            do = do_ref[base + first : base + seg]
+            k = k_ref[start : start + size]
+            s = dot(k, q, NT) * EXP2_SCALE - lse_row[:, first:]
+            if kind == "mem":
+                slot = start + lax.broadcasted_iota(jnp.int32, s.shape, 0)
+                s = jnp.where(slot >= off_ref[0], s, masked_score)
+            else:
+                key = lax.broadcasted_iota(jnp.int32, s.shape, 0)
+                row = lax.broadcasted_iota(jnp.int32, s.shape, 1)
+                s = jnp.where(key <= row, s, masked_score)
+            p = jnp.exp2(s)
+            dp = dot(v_ref[start : start + size], do, NT)
+            ds = (p * (dp - delta_row[:, first:])).astype(BF16)
+            dv_ref[start : start + size] = dot(p.astype(BF16), do).astype(BF16)
+            dk_ref[start : start + size] = (dot(ds, q) * SCALE).astype(BF16)
+            dq = dot(ds, k, TN)
+            if first == 0:
+                dq_low = dq_low + dq[:half]
+                dq_high = dq_high + dq[half:]
+            else:
+                dq_high = dq_high + dq
+        dq_ref[base : base + half] = (dq_low * SCALE).astype(BF16)
+        dq_ref[base + half : base + seg] = (dq_high * SCALE).astype(BF16)
+
+
+def attn_bwd(first_slot, q, k, v, do, mixed, lse):
+    rows, width = q.shape
+    keys = k.shape[0]
+    q_spec = pl.BlockSpec((rows, HEAD_DIM), lambda h: (0, h))
+    k_spec = pl.BlockSpec((keys, HEAD_DIM), lambda h: (0, h))
+    return pl.pallas_call(
+        attn_bwd_kernel,
+        grid=(HEADS,),
+        out_shape=(
+            jax.ShapeDtypeStruct((rows, width), BF16),
+            jax.ShapeDtypeStruct((keys, width), BF16),
+            jax.ShapeDtypeStruct((keys, width), BF16),
+        ),
+        in_specs=[
+            pl.BlockSpec(memory_space=pltpu.SMEM),
+            q_spec, k_spec, k_spec, q_spec, q_spec, held(lse.shape),
+        ],
+        out_specs=(q_spec, k_spec, k_spec),
+        compiler_params=params(),
+        cost_estimate=cost(25e9, 24e6),
+        name="attn_bwd",
+    )(first_slot, q, k, v, do, mixed, lse)
+
+
+GELU_C = math.sqrt(2.0 / math.pi)
+GELU_A = 0.044715
+CHUNK = 512
+
+
+def add_low(left, right):
+    return (left.astype(F32) + right.astype(F32)).astype(BF16)
+
+
+def mesh_place():
+    rank, core = lax.axis_index("dp"), lax.axis_index("seq")
+
+    def bit(b):
+        return lax.rem(lax.div(rank, 1 << b), 2)
+
+    def across(b):
+        return rank + (1 << b) * (1 - 2 * bit(b))
+
+    return core, bit, across
+
+
+def greet(devices):
+    barrier = pltpu.get_barrier_semaphore()
+    for device in devices:
+        pl.semaphore_signal(
+            barrier, inc=1, device_id=device, device_id_type=pl.DeviceIdType.MESH
+        )
+    pl.semaphore_wait(barrier, len(devices))
+
+
+def remote(src, dst, sems, device):
+    return pltpu.make_async_remote_copy(
+        src_ref=src,
+        dst_ref=dst,
+        send_sem=sems[0],
+        recv_sem=sems[1],
+        device_id=device,
+        device_id_type=pl.DeviceIdType.MESH,
+    )
+
+
+def gelu_pair(pre, act_grad):
+    square = pre * pre
+    t = jnp.tanh(pre * (GELU_C + (GELU_C * GELU_A) * square))
+    cdf = 0.5 + 0.5 * t
+    slope = cdf + (0.5 * pre) * (1.0 - t * t) * (GELU_C + (3.0 * GELU_C * GELU_A) * square)
+    return (pre * cdf).astype(BF16), (act_grad * slope).astype(BF16)
+
+
+def ffn_kernel(
+    x_ref, og_ref, hidden_ref, gain_ref, wo_ref, wh0_ref, wh1_ref, wr0_ref, wr1_ref,
+    out_ref, attn_grad_ref, do_ref, gain_grad_ref,
+    sent_h_ref, kept_h_ref, sent_r_ref, kept_r_ref,
+    out_acc, in_acc, act_ref, pre_ref, core_out, core_in, own_ref, chip_in,
+    core_sems, chip_sems,
+):
+    step = pl.program_id(0)
+    last = pl.num_programs(0) - 1
+    rows, width = x_ref.shape
+    tile = wh0_ref.shape[1]
+    chunks = rows // CHUNK
+    core, bit, across = mesh_place()
+    partner = {"seq": 1 - core}
+    beside = ({"dp": across(0)}, {"dp": across(1)})
+    slot = lax.rem(step, 2)
+
+    def part(m):
+        return pl.ds(pl.multiple_of(m * CHUNK, CHUNK), CHUNK)
+
+    @pl.when(step == 0)
+    def _():
+        greet((partner,) + beside)
+        out_acc[...] = jnp.zeros_like(out_acc)
+        in_acc[...] = jnp.zeros_like(in_acc)
+
+    def core_copy(which, index):
+        return remote(
+            core_out.at[which],
+            core_in.at[which, lax.rem(index, 2)],
+            (core_sems.at[0, which, index], core_sems.at[1, which, index]),
+            partner,
+        )
+
+    def chip_copy(which, index):
+        own = own_ref.at[which, lax.rem(index, 2)]
+        away = 1 - bit(which)
+        src = own.at[:, :, away] if which == 0 else own.at[:, away]
+        return remote(
+            src,
+            chip_in.at[which, index],
+            (chip_sems.at[0, which, index], chip_sems.at[1, which, index]),
+            beside[which],
+        )
+
+    def tile_grads(wh_ref, wr_ref):
+        for m in range(chunks):
+            at = slice(m * CHUNK, (m + 1) * CHUNK)
+            pre = dot(x_ref[at], wh_ref[...])
+            act_grad = dot(og_ref[at], wr_ref[...], NT)
+            act, pre_grad = gelu_pair(pre, act_grad)
+            act_ref[at] = act
+            pre_ref[at] = pre_grad
+            out_acc[at] += dot(act, wr_ref[...])
+            in_acc[at] += dot(pre_grad, wh_ref[...], NT)
+        return (
+            lambda: dot(x_ref[...], pre_ref[...], TN),
+            lambda: dot(og_ref[...], act_ref[...], TN),
+        )
+
+    def settle(index):
+        cols = pl.ds(pl.multiple_of(index * tile, tile), tile)
+        at = lax.rem(index, 2)
+        for which, sent_ref, kept_ref in ((0, sent_h_ref, kept_h_ref), (1, sent_r_ref, kept_r_ref)):
+            chip_copy(which, index).wait()
+            own = own_ref.at[which, at]
+            near = bit(which)
+            mine = own.at[:, :, near] if which == 0 else own.at[:, near]
+            here = bit(1 - which)
+            got = chip_in.at[which, index]
+            kept_ref[:, :, cols] = add_low(mine[:, here], got[:, here])
+            sent_ref[:, :, cols] = add_low(mine[:, 1 - here], got[:, 1 - here])
+
+    grads = tile_grads(wh0_ref, wr0_ref)
+    for which in range(2):
+
+        @pl.when(step > 0)
+        def _():
+            core_copy(which, step - 1).wait_send()
+
+        core_out[which] = grads[which]().astype(BF16)
+        core_copy(which, step).start()
+
+    grads = tile_grads(wh1_ref, wr1_ref)
+
+    @pl.when(step > 0)
+    def _():
+        settle(step - 1)
+
+    for which in range(2):
+        total = grads[which]()
+        core_copy(which, step).wait_recv()
+        total = (total + core_in[which, slot].astype(F32)).astype(BF16)
+        own_ref[which, slot] = total.reshape(own_ref.shape[2:])
+        chip_copy(which, step).start()
+
+    @pl.when(step == last)
+    def _():
+        def finish(m, gain_sum):
+            at = pl.ds(pl.multiple_of(m * 256, 256), 256)
+            hidden = hidden_ref[at, :]
+            out_ref[at, :] = (hidden + out_acc[at, :]).astype(BF16)
+            unit, inverse = norm_parts(hidden)
+            grad = in_acc[at, :]
+            hidden_grad = og_ref[at, :].astype(F32) + norm_back(
+                grad * gain_ref[...], unit, inverse
+            )
+            low = hidden_grad.astype(BF16)
+            attn_grad_ref[at, :] = low
+            do_ref[at, :] = dot(low, wo_ref[...], NT).astype(BF16)
+            return gain_sum + jnp.sum(grad * unit, axis=0, keepdims=True)
+
+        gain_grad_ref[...] = lax.fori_loop(
+            0, rows // 256, finish, jnp.zeros(gain_grad_ref.shape, F32)
+        )
+        settle(last)
+        for which in range(2):
+            core_copy(which, step).wait_send()
+
+
+def ffn(x, og, hidden, gain, wo, wh0, wh1, wr0, wr1):
+    rows, width = x.shape
+    units = wh0.shape[1]
+    tile = 512
+    steps = units // tile
+    count = lax.axis_size("dp")
+    block = width // count
+    col = pl.BlockSpec((width, tile), lambda i: (0, i))
+    row = pl.BlockSpec((tile, width), lambda i: (i, 0))
+    whole = held((rows, width))
+    quarter = (count // 4, block, units)
+    low_rows = jax.ShapeDtypeStruct((rows, width), BF16)
+    low_quarter = jax.ShapeDtypeStruct(quarter, BF16)
+    return pl.pallas_call(
+        ffn_kernel,
+        grid=(steps,),
+        out_shape=(
+            low_rows, low_rows, low_rows, jax.ShapeDtypeStruct((1, width), F32),
+            low_quarter, low_quarter, low_quarter, low_quarter,
+        ),
+        in_specs=[whole, whole, whole, held(gain.shape), held(wo.shape), col, col, row, row],
+        out_specs=(whole, whole, whole, held((1, width))) + (held(quarter),) * 4,
+        scratch_shapes=[
+            pltpu.VMEM((rows, width), F32),
+            pltpu.VMEM((rows, width), F32),
+            pltpu.VMEM((rows, tile), BF16),
+            pltpu.VMEM((rows, tile), BF16),
+            pltpu.VMEM((2, width, tile), BF16),
+            pltpu.VMEM((2, 2, width, tile), BF16),
+            pltpu.VMEM((2, 2, count // 4, 2, 2, block, tile), BF16),
+            pltpu.VMEM((2, steps, count // 4, 2, block, tile), BF16),
+            pltpu.SemaphoreType.DMA((2, 2, steps)),
+            pltpu.SemaphoreType.DMA((2, 2, steps)),
+        ],
+        compiler_params=pltpu.CompilerParams(
+            vmem_limit_bytes=VMEM_LIMIT, dimension_semantics=("arbitrary",),
+            collective_id=1, has_side_effects=True,
+        ),
+        cost_estimate=cost(75e9, 50e6),
+        name="ffn",
+    )(x, og, hidden, gain, wo, wh0, wh1, wr0, wr1)
+
+
+def swap_dp(block, bit):
+    count = lax.axis_size("dp")
+    return lax.ppermute(block, "dp", [(i, i ^ (1 << bit)) for i in range(count)])
+
+
+def swap_core(block):
+    return lax.ppermute(block, "seq", [(0, 1), (1, 0)])
+
+
+def reduce_chips(own, other, order, left=(3, 2, 1, 0)):
+    rank = lax.axis_index("dp")
+    bits = len(left)
+    shape = own.shape[1:]
+    left = list(left)
+    own = own.reshape((2,) * bits + shape)
+    other = other.reshape((2,) * bits + shape)
+    for bit in order:
+        axis = left.index(bit)
+        left.remove(bit)
+        mine = (rank >> bit) & 1
+
+        def half(which):
+            pick = functools.partial(lax.dynamic_index_in_dim, axis=axis, keepdims=False)
+            return add_low(pick(own, which), pick(other, which))
+
+        sent = half(1 - mine)
+        own = half(mine)
+        other = swap_dp(sent, bit)
+    return own.astype(F32) + other.astype(F32)
+
+
+def reduce_gains(parts):
+    rank = lax.axis_index("dp")
+    parts = parts + swap_core(parts)
+    for bit in range(lax.axis_size("dp").bit_length() - 1):
+        parts = parts + swap_dp(parts, bit)
+    return lax.dynamic_index_in_dim(parts, rank, 0, False)
+
+
+def on_device_pair(
+    inputs, memory, compressed, offsets, resets, w_query, w_key, w_value, w_output, w_hidden,
+    w_return, w_compress, gain_attn, gain_ffn, out_grad, comp_grad,
+):
+    core = lax.axis_index("seq")
+    dp_count = lax.axis_size("dp")
+    streams, half, width = inputs.shape
+    seg = 2 * half
+    low_core = core == 0
+
+    unused = (resets != 0) | (offsets >= 2 * seg)
+
+    def pair(which):
+        first_unused = lax.dynamic_index_in_dim(unused, which, 0, False)
+        return jnp.where(first_unused, which + 2, which), jnp.where(first_unused, which, which + 2)
+
+    mine, theirs = pair(core), pair(1 - core)
+
+    def take(array, index):
+        return lax.dynamic_index_in_dim(array, index, 0, False)
+
+    def rows_of(which):
+        a, b = which
+        return jnp.stack(
+            [take(compressed, a), take(memory, a), take(inputs, a), take(inputs, b),
+             take(memory, b), take(out_grad, a), take(out_grad, b)]
+        )
+
+    sent = rows_of(theirs)
+    got = swap_core(sent)
+    kept = rows_of(mine)
+    whole = jnp.concatenate(
+        [jnp.where(low_core, kept, got), jnp.where(low_core, got, kept)], axis=1
+    )
+    wh_other, wr_other = swap_core(w_hidden), swap_core(w_return)
+
+    all_rows = whole[:4].reshape(4 * seg, width)
+    in_rows = whole[2:4].reshape(2 * seg, width)
+    og = whole[5:7].reshape(2 * seg, width)
+    reset_a, reset_b = take(resets, mine[0]), take(resets, mine[1])
+    first_slot = jnp.where(reset_a != 0, 2 * seg, take(offsets, mine[0])).reshape(1)
+
+    gain_a = gain_attn.astype(F32).reshape(1, width)
+    gain_f = gain_ffn.astype(F32).reshape(1, width)
+    normed_unit, normed_inverse = norm_parts(all_rows.astype(F32))
+    normed = (normed_unit * gain_a).astype(BF16)
+    q = dot(normed[2 * seg :], w_query).astype(BF16)
+    k = dot(normed, w_key).astype(BF16)
+    v = dot(normed, w_value).astype(BF16)
+
+    groups = comp_grad.shape[1]
+    keep_pair = jnp.stack([reset_a == 0, reset_b == 0]).astype(BF16)
+    mem_pair = jnp.stack([whole[1], whole[4]]) * keep_pair[:, None, None]
+    grouped = mem_pair[:, : RATE * groups].reshape(2 * groups, RATE * width)
+    comp_rows = dot(grouped, w_compress).astype(BF16).reshape(2, groups, width)
+    comp_cot = jnp.stack([take(comp_grad, mine[0]), take(comp_grad, mine[1])]).reshape(
+        2 * groups, width
+    )
+
+    def split_cores(grad):
+        cols = grad.reshape(grad.shape[0], 2, grad.shape[1] // 2)
+        return (
+            lax.dynamic_index_in_dim(cols, core, 1, False),
+            lax.dynamic_index_in_dim(cols, 1 - core, 1, False),
+        )
+
+    def by_chip(grad):
+        return grad.reshape(dp_count, grad.shape[0] // dp_count, grad.shape[1])
+
+    orders = ((0, 1, 2, 3), (1, 0, 2, 3))
+
+    def reduce_columns(own, other):
+        own, other = by_chip(own), by_chip(other)
+        cols = own.shape[2] // 2
+        return jnp.concatenate(
+            [
+                reduce_chips(own[:, :, part], other[:, :, part], order)
+                for part, order in zip((slice(0, cols), slice(cols, None)), orders)
+            ],
+            axis=1,
+        )
+
+    compress_part = dot(grouped, comp_cot, TN).astype(BF16)
+    compress_own, compress_sent = split_cores(compress_part)
+    grad_compress = reduce_columns(compress_own, swap_core(compress_sent))
+
+    mixed, hidden, ffn_in, lse = attn_fwd(first_slot, q, k, v, in_rows, w_output, gain_f)
+    outputs, attn_grad, mixed_grad, gain_ffn_grad, sent_h, kept_h, sent_r, kept_r = ffn(
+        ffn_in, og, hidden, gain_f, w_output, wh_other, w_hidden, wr_other, w_return
+    )
+    got_h, got_r = swap_dp(sent_h, 1), swap_dp(sent_r, 0)
+    dq, dk, dv = attn_bwd(first_slot, q, k, v, mixed_grad, mixed, lse)
+    grad_hidden = reduce_chips(kept_h, got_h, (2, 3), (3, 2))
+    grad_return = reduce_chips(kept_r, got_r, (2, 3), (3, 2)).T
+    output_part = dot(mixed, attn_grad, TN).astype(BF16)
+    query_part = dot(normed[2 * seg :], dq, TN).astype(BF16)
+    key_part = dot(normed, dk, TN).astype(BF16)
+    value_part = dot(normed, dv, TN).astype(BF16)
+    parts = [split_cores(part) for part in (query_part, key_part, value_part, output_part)]
+    own = jnp.concatenate([part[0] for part in parts], axis=1)
+    got_parts = swap_core(jnp.concatenate([part[1] for part in parts], axis=1))
+    grads = reduce_columns(own, got_parts)
+    cols = width // 2
+    grad_query, grad_key, grad_value, grad_output = (
+        grads[:, i * cols : (i + 1) * cols] for i in range(4)
+    )
+
+    normed_grad = dot(dk, w_key, NT) + dot(dv, w_value, NT)
+    query_back = dot(dq, w_query, NT)
+    normed_grad = normed_grad.at[2 * seg :].add(query_back)
+    gain_attn_grad = jnp.sum(normed_grad * normed_unit, axis=0)
+    input_unit, input_inverse = norm_parts(in_rows.astype(F32))
+    rows_grad = norm_back(normed_grad[2 * seg :] * gain_a, input_unit, input_inverse)
+    input_grad = (rows_grad + attn_grad.astype(F32)).astype(BF16)
+
+    gains = jnp.stack([gain_attn_grad, gain_ffn_grad.reshape(width)])
+    gains = gains.reshape(2, dp_count, width // dp_count).transpose(1, 0, 2)
+    gains = reduce_gains(gains)
+
+    def to_streams(a, b, which):
+        swapped = lax.dynamic_index_in_dim(unused, which, 0, False)
+        return jnp.where(swapped, b, a), jnp.where(swapped, a, b)
+
+    def spread(own_pair, other_pair):
+        own = to_streams(own_pair[0], own_pair[1], core)
+        other = to_streams(other_pair[0], other_pair[1], 1 - core)
+        return jnp.stack(
+            [
+                jnp.where(low_core, own[0], other[0]),
+                jnp.where(low_core, other[0], own[0]),
+                jnp.where(low_core, own[1], other[1]),
+                jnp.where(low_core, other[1], own[1]),
+            ]
+        )
+
+    def place_rows(rows):
+        halves = rows.reshape(2, 2, half, width)
+        return spread(
+            lax.dynamic_index_in_dim(halves, core, 1, False),
+            swap_core(lax.dynamic_index_in_dim(halves, 1 - core, 1, False)),
+        )
+
+    return (
+        place_rows(outputs),
+        spread(comp_rows, swap_core(comp_rows)),
+        place_rows(input_grad),
+        grad_query,
+        grad_key,
+        grad_value,
+        grad_output,
+        grad_hidden,
+        grad_return,
+        grad_compress,
+        gains[0],
+        gains[1],
+    )
+
+
 def solution(mesh):
     placed = (
         P("dp", "seq", None),
@@ -317,8 +923,9 @@
         P("dp", "seq", None),
         P("dp", None, None),
     )
+    fast = mesh.shape["seq"] == 2 and mesh.shape["dp"] == 16
     return jax.shard_map(
-        on_device,
+        on_device_pair if fast else on_device,
         mesh=mesh,
         in_specs=placed,
         out_specs=(

time: 1420 us -> 494 us (0.35)
  waiting for transfers between devices: 720 us -> 89.8 us
  matrix products: 373 us -> 83.4 us
  Pallas kernels: 0 us -> 147 us
  other arithmetic: 116 us -> 52.3 us
  local copies, waits for them, and re-layouts: 140 us -> 76.6 us
  blocking collectives: 40.7 us -> 0 us
  starting transfers between devices: 2.13 us -> 32.2 us
    reduce_scatter x10 -> x0, waiting for transfers between devices: 701 us -> none  [the longest x1 143 us: on_device(): lax.psum_scatter(tile_matrix(output_part, dp_count, seq_count), ('dp', 's...]
    dot_general x26 -> x12, matrix products: 373 us -> 83.4 us  [dot(): return lax.dot_general(left, right, dims, preferred_element_type=F32)]
    pallas_call x0 -> x3, Pallas kernels: none -> 147 us  [the longest x1 90.3 us: ffn(): pl.pallas_call(ffn_kernel, grid=(steps,), out_shape=(low_rows, low_rows,...]
    ppermute x1 -> x35, waiting for transfers between devices: 1.78 us -> 89.8 us  [the longest x26 89.8 us: swap_dp(): return lax.ppermute(block, 'dp', [(i, i ^ 1 << bit) for i in range(count)])]
    convert_element_type x10 -> x30, other arithmetic: 54.3 us -> 9.6 us  [the longest x27 6.38 us: add_low(): return (left.astype(F32) + right.astype(F32)).astype(BF16)]
    unnamed x1 -> x0, blocking collectives: 40.7 us -> none
    reduce_sum x7 -> x5, other arithmetic: 48.7 us -> 11 us  [the longest x2 5.28 us: norm_parts(): jnp.mean(centred * centred, axis=-1, keepdims=True) + epsilon]
    reshape x6 -> x4, local copies, waits for them, and re-layouts: 42.9 us -> 6.69 us  [the longest x1 3.96 us: on_device_pair(): grouped = mem_pair[:, :RATE * groups].reshape(2 * groups, RATE * width)]
  transfers between devices with their start and end apart: 17 -> 35, of which waited for: 12 -> 16; matrix products, arithmetic and copies ran while one was open for 33% -> 41% of each run, Pallas kernels for 0% -> 30%
where the time goes in v1:
time: 494 us; the launch traced here: 489 us
  Pallas kernels  147 us (30%)
  waiting for transfers between devices  89.8 us (18%)
  matrix products  83.4 us (17%)
  local copies, waits for them, and re-layouts  76.6 us (16%)
  other arithmetic  52.3 us (11%)
  starting transfers between devices  32.2 us (7%)
  between operations  7.08 us (1%)
    pallas_call x1, Pallas kernels, ffn(): pl.pallas_call(ffn_kernel, grid=(steps,), out_shape=(low_rows, low_rows,...  90.3 us
    ppermute x26, waiting for transfers between devices, swap_dp(): return lax.ppermute(block, 'dp', [(i, i ^ 1 << bit) for i in range(count)])  89.8 us
    dot_general x12, matrix products, dot(): return lax.dot_general(left, right, dims, preferred_element_type=F32)  83.4 us
    pallas_call x1, Pallas kernels, attn_fwd(): pl.pallas_call(attn_fwd_kernel, grid=(4,), out_shape=(jax.ShapeDtypeStruc...  31.3 us
    ppermute x26, starting transfers between devices, swap_dp(): return lax.ppermute(block, 'dp', [(i, i ^ 1 << bit) for i in range(count)])  29.6 us
    unnamed x116, local copies, waits for them, and re-layouts  27.5 us
    pallas_call x1, Pallas kernels, attn_bwd(): pl.pallas_call(attn_bwd_kernel, grid=(HEADS,), out_shape=(jax.ShapeDtypeS...  25.7 us
    dynamic_slice x5, local copies, waits for them, and re-layouts, split_cores(): lax.dynamic_index_in_dim(cols, 1 - core, 1, False)  12.9 us
  transfers between devices with their start and end apart: 35, of which 16 were waited for; matrix products, arithmetic and copies ran while one was open for 41% of the time, Pallas kernels for 30%

profile of v1, /device:TPU:0, one launch (start us, length us, event | category | flops | bytes accessed | tf_op | source)
XLA Modules:
  0.0 488.7 jit_solution(4976832143080275431)
XLA Ops:
  24.4 3.6 broadcast_select_fusion.1
  35.8 4.0 reshape.625
  39.8 5.8 %convolution_convert_fusion.8 = bf16[340,1024]{1,0:T(8,128)(2,1)S(1)} fusion(bf16[340,3072]{1,0:T(8,128)(2,1)} %reshape.625, bf16[3072,1024]{1,0:T(8,128)(2,1)} %param.29), kind=kOutput, calls=%fused_computation.65 | convolution fusion | flops 2139443200 | bytes 9076736 | tf_op jit(solution)/shard_map/dot_general | solution.py:317
  54.0 3.8 convolution_convert_fusion
  60.8 4.7 copy.105
  65.9 3.1 multiply_convert_fusion
  69.1 3.7 convolution_convert_fusion.7.q_ref
  72.8 4.7 copy.131
  77.5 4.0 fusion.84
  81.5 20.7 %convolution_convert_fusion.1.v_ref = bf16[2048,1024]{1,0:T(8,128)(2,1)} fusion(bf16[2048,1024]{1,0:T(8,128)(2,1)S(1)} %copy-done.14, bf16[1024,1024]{1,0:T(8,128)(2,1)S(1)} %copy-done), kind=kOutput, calls=%fused_computation.29 | convolution fusion | flops 4297064448 | bytes 10485760 | tf_op jit(solution)/shard_map/dot_general | solution.py:317
  102.2 6.0 %convolution_convert_fusion.2.k_ref = bf16[2048,1024]{1,0:T(8,128)(2,1)} fusion(bf16[2048,1024]{1,0:T(8,128)(2,1)S(1)} %copy-done.14, bf16[1024,1024]{1,0:T(8,128)(2,1)S(1)} %copy-done.41), kind=kOutput, calls=%fused_computation.30 | convolution fusion | flops 4297064448 | bytes 10485760 | tf_op jit(solution)/shard_map/dot_general | solution.py:317
  108.2 31.3 %attn_fwd.1 = (bf16[1024,1024]{1,0:T(8,128)(2,1)}, f32[1024,1024]{1,0:T(8,128)}, bf16[1024,1024]{1,0:T(8,128)(2,1)}, f32[8,1024]{1,0:T(8,128)}) custom-call(s32[1]{0:T(128)S(6)} %select_n.389.off_ref, bf16[1024,1024]{1,0:T(8,128)(2,1)} %convolution_convert_fusion.7.q_ref, bf16[2048,1024]{1,0:T(8,128)(2,1)} %convolution_convert_fusion.2.k_ref, ...), custom_call_target="tpu_custom_call" | custom-call | flops 20000000000 | bytes 20000000 | tf_op jit(solution)/shard_map/attn_fwd/pallas_call | solution.py:408
  139.5 90.3 %ffn.1 = (bf16[1024,1024]{1,0:T(8,128)(2,1)}, bf16[1024,1024]{1,0:T(8,128)(2,1)}, bf16[1024,1024]{1,0:T(8,128)(2,1)}, f32[1,1024]{1,0:T(1,128)}, bf16[4,64,2048]...) custom-call(bf16[1024,1024]{1,0:T(8,128)(2,1)} %get-tuple-element.39., ...), custom_call_target="tpu_custom_call" | custom-call | flops 74999996416 | bytes 50000000 | tf_op jit(solution)/shard_map/ffn/pallas_call | solution.py:680
  229.8 25.7 %attn_bwd.1 = (bf16[1024,1024]{1,0:T(8,128)(2,1)}, bf16[2048,1024]{1,0:T(8,128)(2,1)}, bf16[2048,1024]{1,0:T(8,128)(2,1)}) custom-call(s32[1]{0:T(128)S(6)} %select_n.389.off_ref, bf16[1024,1024]{1,0:T(8,128)(2,1)} %convolution_convert_fusion.7.q_ref, bf16[2048,1024]{1,0:T(8,128)(2,1)} %convolution_convert_fusion.2.k_ref, ...), custom_call_target="tpu_custom_call" | custom-call | flops 24999999488 | bytes 24000000 | tf_op jit(solution)/shard_map/attn_bwd/pallas_call | solution.py:479
  255.5 9.4 %convolution_convert_fusion.4 = bf16[1024,1024]{0,1:T(8,128)(2,1)} fusion(bf16[2048,1024]{1,0:T(8,128)(2,1)} %copy-done.13, bf16[2048,1024]{1,0:T(8,128)(2,1)} %get-tuple-element.46), kind=kOutput, calls=%fused_computation.54 | convolution fusion | flops 4296015872 | bytes 10485760 | tf_op jit(solution)/shard_map/dot_general | solution.py:317
  265.0 7.1 %fusion.91 = f32[2048,1024]{1,0:T(8,128)} fusion(bf16[2048,1024]{1,0:T(8,128)(2,1)S(1)} %copy-done.49, bf16[1024,1024]{1,0:T(8,128)(2,1)S(1)} %copy-done), kind=kOutput, calls=%fused_computation.262 | convolution fusion | flops 4294967296 | bytes 14680064 | tf_op jit(solution)/shard_map/dot_general | solution.py:317
  272.2 3.8 convolution_convert_fusion.3
  277.2 9.5 %convolution_convert_fusion.5 = bf16[1024,1024]{0,1:T(8,128)(2,1)} fusion(bf16[2048,1024]{1,0:T(8,128)(2,1)} %copy-done.13, bf16[2048,1024]{1,0:T(8,128)(2,1)} %get-tuple-element.45), kind=kOutput, calls=%fused_computation.55 | convolution fusion | flops 4296015872 | bytes 10485760 | tf_op jit(solution)/shard_map/dot_general | solution.py:317
  286.7 3.8 convolution_convert_fusion.6
  291.5 6.8 %convolution_add_fusion = f32[2048,1024]{1,0:T(8,128)S(1)} fusion(f32[2048,1024]{1,0:T(8,128)S(1)} %copy-done.46, bf16[2048,1024]{1,0:T(8,128)(2,1)} %get-tuple-element.45, bf16[1024,1024]{1,0:T(8,128)(2,1)S(1)} %copy-done.42), kind=kOutput, calls=%fused_computation.28 | convolution fusion | flops 4297064448 | bytes 23068672 | tf_op jit(solution)/shard_map/dot_general | solution.py:317
  298.3 3.1 multiply_reduce_fusion.3
  311.1 4.1 constant_dynamic-slice_fusion.12
  326.7 7.9 %collective-permute-done.32 = f32[16,2,64]{2,1,0:T(2,128)S(1)} collective-permute-done((f32[16,2,64]{2,1,0:T(2,128)S(1)}, f32[16,2,64]{2,1,0:T(2,128)S(1)}, u32[]{:S(2)}, u32[]{:S(2)}) %collective-permute-start.32) | collective-permute-done | bytes 8224 | tf_op jit(solution)/shard_map/ppermute | solution.py:712
  336.3 3.9 pad_maximum_fusion
  365.0 11.7 %collective-permute-done.18 = bf16[4,64,2048]{2,1,0:T(8,128)(2,1)S(1)} collective-permute-done((bf16[4,64,2048]{2,1,0:T(8,128)(2,1)}, bf16[4,64,2048]{2,1,0:T(8,128)(2,1)S(1)}, u32[]{:S(2)}, u32[]{:S(2)}) %collective-permute-start.18) | collective-permute-done | bytes 1048608 | tf_op jit(solution)/shard_map/ppermute | solution.py:712
  386.5 7.9 %collective-permute-done.16 = bf16[2,64,2048]{2,1,0:T(8,128)(2,1)S(1)} collective-permute-done((bf16[2,64,2048]{2,1,0:T(8,128)(2,1)S(1)}, bf16[2,64,2048]{2,1,0:T(8,128)(2,1)S(1)}, u32[]{:S(2)}, u32[]{:S(2)}) %collective-permute-start.16) | collective-permute-done | bytes 524320 | tf_op jit(solution)/shard_map/ppermute | solution.py:712
  394.5 9.7 %collective-permute-done.19 = bf16[2,64,2048]{2,1,0:T(8,128)(2,1)S(1)} collective-permute-done((bf16[2,64,2048]{2,1,0:T(8,128)(2,1)S(1)}, bf16[2,64,2048]{2,1,0:T(8,128)(2,1)S(1)}, u32[]{:S(2)}, u32[]{:S(2)}) %collective-permute-start.19) | collective-permute-done | bytes 524320 | tf_op jit(solution)/shard_map/ppermute | solution.py:712
  410.2 13.2 %collective-permute-done.22 = bf16[2,2,2,192,256]{4,3,2,1,0:T(8,128)(2,1)S(1)} collective-permute-done((bf16[2,2,2,192,256]{4,3,2,1,0:T(8,128)(2,1)S(1)}, bf16[2,2,2,192,256]{4,3,2,1,0:T(8,128)(2,1)S(1)}, u32[]{:S(2)}, u32[]{:S(2)}) %collective-permute-start.22) | collective-permute-done | bytes 786464 | tf_op jit(solution)/shard_map/ppermute | solution.py:712
  445.8 13.2 %collective-permute-done.11 = bf16[2,2,2,64,1024]{4,3,2,1,0:T(8,128)(2,1)S(1)} collective-permute-done((bf16[2,2,2,64,1024]{4,3,2,1,0:T(8,128)(2,1)S(1)}, bf16[2,2,2,64,1024]{4,3,2,1,0:T(8,128)(2,1)S(1)}, u32[]{:S(2)}, u32[]{:S(2)}) %collective-permute-start.11) | collective-permute-done | bytes 1048608 | tf_op jit(solution)/shard_map/ppermute | solution.py:712
  465.0 4.0 collective-permute-done.12
  469.7 3.1 collective-permute-done.8
  473.6 3.7 collective-permute-done.13
  (272 shorter events, 144.3 us)
Async XLA Ops:
  14.7 9.7 %collective-permute-start = (bf16[7,256,1024]{2,1,0:T(8,128)(2,1)}, bf16[7,256,1024]{2,1,0:T(8,128)(2,1)}, u32[]{:S(2)}, u32[]{:S(2)}) collective-permute-start(bf16[7,256,1024]{2,1,0:T(8,128)(2,1)} %get-tuple-element.135), channel_id=1, source_target_pairs={{0,1},{1,0},{2,3},{3,2},{4,5},{5,4},{6,7},{7,6},{8,9},{9,8},{10,11... | collective-permute-start | bytes 11010056 | tf_op jit(solution)/shard_map/ppermute | solution.py:716
  15.2 124.3 %collective-permute-start.1 = (bf16[1024,2048]{1,0:T(8,128)(2,1)}, bf16[1024,2048]{1,0:T(8,128)(2,1)}, u32[]{:S(2)}, u32[]{:S(2)}) collective-permute-start(bf16[1024,2048]{1,0:T(8,128)(2,1)} %wh1_ref.1), channel_id=1, source_target_pairs={{0,1},{1,0},{2,3},{3,2},{4,5},{5,4},{6,7},{7,6},{8,9},{9,8},{10,11... | collective-permute-start | bytes 12582920 | tf_op jit(solution)/shard_map/ppermute | solution.py:716
  15.3 124.2 %collective-permute-start.2 = (bf16[2048,1024]{1,0:T(8,128)(2,1)}, bf16[2048,1024]{1,0:T(8,128)(2,1)}, u32[]{:S(2)}, u32[]{:S(2)}) collective-permute-start(bf16[2048,1024]{1,0:T(8,128)(2,1)} %wr1_ref.1), channel_id=1, source_target_pairs={{0,1},{1,0},{2,3},{3,2},{4,5},{5,4},{6,7},{7,6},{8,9},{9,8},{10,11... | collective-permute-start | bytes 12582920 | tf_op jit(solution)/shard_map/ppermute | solution.py:716
  47.3 307.0 %collective-permute-start.4 = (bf16[2,170,1024]{2,0,1:T(2,128)(2,1)}, bf16[2,170,1024]{2,0,1:T(2,128)(2,1)}, u32[]{:S(2)}, u32[]{:S(2)}) collective-permute-start(bf16[2,170,1024]{2,0,1:T(2,128)(2,1)} %copy.81), channel_id=1, source_target_pairs={{0,1},{1,0},{2,3},{3,2},{4,5},{5,4},{6,7},{7,6},{8,9},{9,8},{10,11... | collective-permute-start | bytes 2088968 | tf_op jit(solution)/shard_map/ppermute | solution.py:716
  65.5 339.0 %collective-permute-start.21 = (bf16[3072,512]{1,0:T(8,128)(2,1)}, bf16[3072,512]{1,0:T(8,128)(2,1)}, u32[]{:S(2)}, u32[]{:S(2)}) collective-permute-start(bf16[3072,512]{1,0:T(8,128)(2,1)} %bitcast.329), channel_id=1, source_target_pairs={{0,1},{1,0},{2,3},{3,2},{4,5},{5,4},{6,7},{7,6},{8,9},{9,8},{10,11... | collective-permute-start | bytes 9437192 | tf_op jit(solution)/shard_map/ppermute | solution.py:716
  308.5 69.0 %collective-permute-start.3 = (bf16[2,256,1024]{2,1,0:T(8,128)(2,1)}, bf16[2,256,1024]{2,1,0:T(8,128)(2,1)}, u32[]{:S(2)}, u32[]{:S(2)}) collective-permute-start(bf16[2,256,1024]{2,1,0:T(8,128)(2,1)} %dynamic-slice_bitcast_fusion.1), channel_id=1, source_target_pairs={{0,1},{1,0},{2,3},{3,2},{4,5},{5,4},{6,7},{7,6},{8,9},{9,8},{10,11... | collective-permute-start | bytes 3145736 | tf_op jit(solution)/shard_map/ppermute | solution.py:716
  309.0 53.8 %collective-permute-start.15 = (bf16[4,64,2048]{2,1,0:T(8,128)(2,1)}, bf16[4,64,2048]{2,1,0:T(8,128)(2,1)}, u32[]{:S(2)}, u32[]{:S(2)}) collective-permute-start(bf16[4,64,2048]{2,1,0:T(8,128)(2,1)} %get-tuple-element.50), channel_id=1, source_target_pairs={{0,4},{2,6},{4,0},{6,2},{8,12},{10,14},{12,8},{14,10},{16,20},{18,... | collective-permute-start | bytes 3145736 | tf_op jit(solution)/shard_map/ppermute | solution.py:712
  315.3 19.4 %collective-permute-start.32 = (f32[16,2,64]{2,1,0:T(2,128)S(1)}, f32[16,2,64]{2,1,0:T(2,128)S(1)}, u32[]{:S(2)}, u32[]{:S(2)}) collective-permute-start(f32[16,2,64]{2,1,0:T(2,128)S(1)} %fusion.114), channel_id=1, source_target_pairs={{0,4},{2,6},{4,0},{6,2},{8,12},{10,14},{12,8},{14,10},{16,20},{18,... | collective-permute-start | bytes 24584 | tf_op jit(solution)/shard_map/ppermute | solution.py:712
  340.3 12.4 %collective-permute-start.34 = (f32[16,2,64]{2,1,0:T(2,128)S(1)}, f32[16,2,64]{2,1,0:T(2,128)S(1)}, u32[]{:S(2)}, u32[]{:S(2)}) collective-permute-start(f32[16,2,64]{2,1,0:T(2,128)S(1)} %add.488), channel_id=1, source_target_pairs={{0,16},{2,18},{4,20},{6,22},{8,24},{10,26},{12,28},{14,30},{16,0},... | collective-permute-start | bytes 24584 | tf_op jit(solution)/shard_map/ppermute | solution.py:712
  352.6 24.1 %collective-permute-start.18 = (bf16[4,64,2048]{2,1,0:T(8,128)(2,1)}, bf16[4,64,2048]{2,1,0:T(8,128)(2,1)S(1)}, u32[]{:S(2)}, u32[]{:S(2)}) collective-permute-start(bf16[4,64,2048]{2,1,0:T(8,128)(2,1)} %get-tuple-element.52), channel_id=1, source_target_pairs={{0,2},{2,0},{4,6},{6,4},{8,10},{10,8},{12,14},{14,12},{16,18},{18,... | collective-permute-start | bytes 3145736 | tf_op jit(solution)/shard_map/ppermute | solution.py:712
  354.3 27.6 %collective-permute-start.5 = (bf16[2,256,1024]{2,1,0:T(8,128)(2,1)}, bf16[2,256,1024]{2,1,0:T(8,128)(2,1)S(1)}, u32[]{:S(2)}, u32[]{:S(2)}) collective-permute-start(bf16[2,256,1024]{2,1,0:T(8,128)(2,1)} %dynamic-slice_bitcast_fusion), channel_id=1, source_target_pairs={{0,1},{1,0},{2,3},{3,2},{4,5},{5,4},{6,7},{7,6},{8,9},{9,8},{10,11... | collective-permute-start | bytes 3145736 | tf_op jit(solution)/shard_map/ppermute | solution.py:716
  362.8 74.0 %collective-permute-start.6 = (bf16[1024,2048]{1,0:T(8,128)(2,1)S(1)}, bf16[1024,2048]{1,0:T(8,128)(2,1)S(1)}, u32[]{:S(2)}, u32[]{:S(2)}) collective-permute-start(bf16[1024,2048]{1,0:T(8,128)(2,1)S(1)} %copy-done.12), channel_id=1, source_target_pairs={{0,1},{1,0},{2,3},{3,2},{4,5},{5,4},{6,7},{7,6},{8,9},{9,8},{10,11... | collective-permute-start | bytes 12582920 | tf_op jit(solution)/shard_map/ppermute | solution.py:716
  376.7 17.7 %collective-permute-start.16 = (bf16[2,64,2048]{2,1,0:T(8,128)(2,1)S(1)}, bf16[2,64,2048]{2,1,0:T(8,128)(2,1)S(1)}, u32[]{:S(2)}, u32[]{:S(2)}) collective-permute-start(bf16[2,64,2048]{2,1,0:T(8,128)(2,1)S(1)} %get-tuple-element.123), channel_id=1, source_target_pairs={{0,8},{2,10},{4,12},{6,14},{8,0},{10,2},{12,4},{14,6},{16,24},{18,... | collective-permute-start | bytes 1572872 | tf_op jit(solution)/shard_map/ppermute | solution.py:712
  377.5 26.7 %collective-permute-start.19 = (bf16[2,64,2048]{2,1,0:T(8,128)(2,1)S(1)}, bf16[2,64,2048]{2,1,0:T(8,128)(2,1)S(1)}, u32[]{:S(2)}, u32[]{:S(2)}) collective-permute-start(bf16[2,64,2048]{2,1,0:T(8,128)(2,1)S(1)} %get-tuple-element.121), channel_id=1, source_target_pairs={{0,8},{2,10},{4,12},{6,14},{8,0},{10,2},{12,4},{14,6},{16,24},{18,... | collective-permute-start | bytes 1572872 | tf_op jit(solution)/shard_map/ppermute | solution.py:712
  394.5 34.0 %collective-permute-start.17 = (bf16[64,2048]{1,0:T(8,128)(2,1)S(1)}, bf16[64,2048]{1,0:T(8,128)(2,1)S(1)}, u32[]{:S(2)}, u32[]{:S(2)}) collective-permute-start(bf16[64,2048]{1,0:T(8,128)(2,1)S(1)} %fusion.56), channel_id=1, source_target_pairs={{0,16},{2,18},{4,20},{6,22},{8,24},{10,26},{12,28},{14,30},{16,0},... | collective-permute-start | bytes 786440 | tf_op jit(solution)/shard_map/ppermute | solution.py:712
  404.3 36.7 %collective-permute-start.20 = (bf16[64,2048]{1,0:T(8,128)(2,1)S(1)}, bf16[64,2048]{1,0:T(8,128)(2,1)S(1)}, u32[]{:S(2)}, u32[]{:S(2)}) collective-permute-start(bf16[64,2048]{1,0:T(8,128)(2,1)S(1)} %fusion.58), channel_id=1, source_target_pairs={{0,16},{2,18},{4,20},{6,22},{8,24},{10,26},{12,28},{14,30},{16,0},... | collective-permute-start | bytes 786440 | tf_op jit(solution)/shard_map/ppermute | solution.py:712
  407.0 16.4 %collective-permute-start.22 = (bf16[2,2,2,192,256]{4,3,2,1,0:T(8,128)(2,1)S(1)}, bf16[2,2,2,192,256]{4,3,2,1,0:T(8,128)(2,1)S(1)}, u32[]{:S(2)}, u32[]{:S(2)}) collective-permute-start(bf16[2,2,2,192,256]{4,3,2,1,0:T(8,128)(2,1)S(1)} %fusion.24), channel_id=1, source_target_pairs={{0,2},{2,0},{4,6},{6,4},{8,10},{10,8},{12,14},{14,12},{16,18},{18,... | collective-permute-start | bytes 2359304 | tf_op jit(solution)/shard_map/ppermute | solution.py:712
  408.6 18.6 %collective-permute-start.26 = (bf16[2,2,2,192,256]{4,3,0,2,1:T(8,128)(2,1)S(1)}, bf16[2,2,2,192,256]{4,3,0,2,1:T(8,128)(2,1)S(1)}, u32[]{:S(2)}, u32[]{:S(2)}) collective-permute-start(bf16[2,2,2,192,256]{4,3,0,2,1:T(8,128)(2,1)S(1)} %fusion.25), channel_id=1, source_target_pairs={{0,4},{2,6},{4,0},{6,2},{8,12},{10,14},{12,8},{14,10},{16,20},{18,... | collective-permute-start | bytes 2359304 | tf_op jit(solution)/shard_map/ppermute | solution.py:712
  423.5 7.9 %collective-permute-start.23 = (bf16[2,2,192,256]{3,2,1,0:T(8,128)(2,1)S(1)}, bf16[2,2,192,256]{3,2,1,0:T(8,128)(2,1)S(1)}, u32[]{:S(2)}, u32[]{:S(2)}) collective-permute-start(bf16[2,2,192,256]{3,2,1,0:T(8,128)(2,1)S(1)} %fusion.43), channel_id=1, source_target_pairs={{0,4},{2,6},{4,0},{6,2},{8,12},{10,14},{12,8},{14,10},{16,20},{18,... | collective-permute-start | bytes 1179656 | tf_op jit(solution)/shard_map/ppermute | solution.py:712
  427.4 8.6 %collective-permute-start.27 = (bf16[2,2,192,256]{3,2,1,0:T(8,128)(2,1)S(1)}, bf16[2,2,192,256]{3,2,1,0:T(8,128)(2,1)S(1)}, u32[]{:S(2)}, u32[]{:S(2)}) collective-permute-start(bf16[2,2,192,256]{3,2,1,0:T(8,128)(2,1)S(1)} %copy.115), channel_id=1, source_target_pairs={{0,2},{2,0},{4,6},{6,4},{8,10},{10,8},{12,14},{14,12},{16,18},{18,... | collective-permute-start | bytes 1179656 | tf_op jit(solution)/shard_map/ppermute | solution.py:712
  431.5 10.4 %collective-permute-start.24 = (bf16[2,192,256]{2,1,0:T(8,128)(2,1)S(1)}, bf16[2,192,256]{2,1,0:T(8,128)(2,1)S(1)}, u32[]{:S(2)}, u32[]{:S(2)}) collective-permute-start(bf16[2,192,256]{2,1,0:T(8,128)(2,1)S(1)} %get-tuple-element.161), channel_id=1, source_target_pairs={{0,8},{2,10},{4,12},{6,14},{8,0},{10,2},{12,4},{14,6},{16,24},{18,... | collective-permute-start | bytes 589832 | tf_op jit(solution)/shard_map/ppermute | solution.py:712
  436.2 8.0 %collective-permute-start.28 = (bf16[2,192,256]{2,1,0:T(8,128)(2,1)S(1)}, bf16[2,192,256]{2,1,0:T(8,128)(2,1)S(1)}, u32[]{:S(2)}, u32[]{:S(2)}) collective-permute-start(bf16[2,192,256]{2,1,0:T(8,128)(2,1)S(1)} %get-tuple-element.163), channel_id=1, source_target_pairs={{0,8},{2,10},{4,12},{6,14},{8,0},{10,2},{12,4},{14,6},{16,24},{18,... | collective-permute-start | bytes 589832 | tf_op jit(solution)/shard_map/ppermute | solution.py:712
  438.4 20.5 %collective-permute-start.11 = (bf16[2,2,2,64,1024]{4,3,2,1,0:T(8,128)(2,1)S(1)}, bf16[2,2,2,64,1024]{4,3,2,1,0:T(8,128)(2,1)S(1)}, u32[]{:S(2)}, u32[]{:S(2)}) collective-permute-start(bf16[2,2,2,64,1024]{4,3,2,1,0:T(8,128)(2,1)S(1)} %fusion.14), channel_id=1, source_target_pairs={{0,4},{2,6},{4,0},{6,2},{8,12},{10,14},{12,8},{14,10},{16,20},{18,... | collective-permute-start | bytes 3145736 | tf_op jit(solution)/shard_map/ppermute | solution.py:712
  439.7 23.6 %collective-permute-start.7 = (bf16[2,2,2,64,1024]{4,3,2,1,0:T(8,128)(2,1)S(1)}, bf16[2,2,2,64,1024]{4,3,2,1,0:T(8,128)(2,1)S(1)}, u32[]{:S(2)}, u32[]{:S(2)}) collective-permute-start(bf16[2,2,2,64,1024]{4,3,2,1,0:T(8,128)(2,1)S(1)} %fusion.13), channel_id=1, source_target_pairs={{0,2},{2,0},{4,6},{6,4},{8,10},{10,8},{12,14},{14,12},{16,18},{18,... | collective-permute-start | bytes 3145736 | tf_op jit(solution)/shard_map/ppermute | solution.py:712
  441.9 22.6 %collective-permute-start.25 = (bf16[192,256]{1,0:T(8,128)(2,1)S(1)}, bf16[192,256]{1,0:T(8,128)(2,1)S(1)}, u32[]{:S(2)}, u32[]{:S(2)}) collective-permute-start(bf16[192,256]{1,0:T(8,128)(2,1)S(1)} %fusion.74), channel_id=1, source_target_pairs={{0,16},{2,18},{4,20},{6,22},{8,24},{10,26},{12,28},{14,30},{16,0},... | collective-permute-start | bytes 294920 | tf_op jit(solution)/shard_map/ppermute | solution.py:712
  444.2 29.3 %collective-permute-start.29 = (bf16[192,256]{1,0:T(8,128)(2,1)S(1)}, bf16[192,256]{1,0:T(8,128)(2,1)S(1)}, u32[]{:S(2)}, u32[]{:S(2)}) collective-permute-start(bf16[192,256]{1,0:T(8,128)(2,1)S(1)} %fusion.76), channel_id=1, source_target_pairs={{0,16},{2,18},{4,20},{6,22},{8,24},{10,26},{12,28},{14,30},{16,0},... | collective-permute-start | bytes 294920 | tf_op jit(solution)/shard_map/ppermute | solution.py:712
  459.2 9.8 %collective-permute-start.12 = (bf16[2,2,64,1024]{3,2,1,0:T(8,128)(2,1)S(1)}, bf16[2,2,64,1024]{3,2,1,0:T(8,128)(2,1)S(1)}, u32[]{:S(2)}, u32[]{:S(2)}) collective-permute-start(bf16[2,2,64,1024]{3,2,1,0:T(8,128)(2,1)S(1)} %fusion.33), channel_id=1, source_target_pairs={{0,2},{2,0},{4,6},{6,4},{8,10},{10,8},{12,14},{14,12},{16,18},{18,... | collective-permute-start | bytes 1572872 | tf_op jit(solution)/shard_map/ppermute | solution.py:712
  463.6 9.2 %collective-permute-start.8 = (bf16[2,2,64,1024]{3,2,1,0:T(8,128)(2,1)S(1)}, bf16[2,2,64,1024]{3,2,1,0:T(8,128)(2,1)S(1)}, u32[]{:S(2)}, u32[]{:S(2)}) collective-permute-start(bf16[2,2,64,1024]{3,2,1,0:T(8,128)(2,1)S(1)} %fusion.32), channel_id=1, source_target_pairs={{0,4},{2,6},{4,0},{6,2},{8,12},{10,14},{12,8},{14,10},{16,20},{18,... | collective-permute-start | bytes 1572872 | tf_op jit(solution)/shard_map/ppermute | solution.py:712
  469.2 8.1 %collective-permute-start.13 = (bf16[2,64,1024]{2,1,0:T(8,128)(2,1)S(1)}, bf16[2,64,1024]{2,1,0:T(8,128)(2,1)S(1)}, u32[]{:S(2)}, u32[]{:S(2)}) collective-permute-start(bf16[2,64,1024]{2,1,0:T(8,128)(2,1)S(1)} %get-tuple-element.157), channel_id=1, source_target_pairs={{0,8},{2,10},{4,12},{6,14},{8,0},{10,2},{12,4},{14,6},{16,24},{18,... | collective-permute-start | bytes 786440 | tf_op jit(solution)/shard_map/ppermute | solution.py:712
  473.0 7.1 %collective-permute-start.9 = (bf16[2,64,1024]{2,1,0:T(8,128)(2,1)S(1)}, bf16[2,64,1024]{2,1,0:T(8,128)(2,1)S(1)}, u32[]{:S(2)}, u32[]{:S(2)}) collective-permute-start(bf16[2,64,1024]{2,1,0:T(8,128)(2,1)S(1)} %get-tuple-element.159), channel_id=1, source_target_pairs={{0,8},{2,10},{4,12},{6,14},{8,0},{10,2},{12,4},{14,6},{16,24},{18,... | collective-permute-start | bytes 786440 | tf_op jit(solution)/shard_map/ppermute | solution.py:712
  477.3 7.3 %collective-permute-start.14 = (bf16[64,1024]{1,0:T(8,128)(2,1)S(1)}, bf16[64,1024]{1,0:T(8,128)(2,1)S(1)}, u32[]{:S(2)}, u32[]{:S(2)}) collective-permute-start(bf16[64,1024]{1,0:T(8,128)(2,1)S(1)} %fusion.72), channel_id=1, source_target_pairs={{0,16},{2,18},{4,20},{6,22},{8,24},{10,26},{12,28},{14,30},{16,0},... | collective-permute-start | bytes 393224 | tf_op jit(solution)/shard_map/ppermute | solution.py:712
  480.2 7.3 %collective-permute-start.10 = (bf16[64,1024]{1,0:T(8,128)(2,1)S(1)}, bf16[64,1024]{1,0:T(8,128)(2,1)S(1)}, u32[]{:S(2)}, u32[]{:S(2)}) collective-permute-start(bf16[64,1024]{1,0:T(8,128)(2,1)S(1)} %fusion.70), channel_id=1, source_target_pairs={{0,16},{2,18},{4,20},{6,22},{8,24},{10,26},{12,28},{14,30},{16,0},... | collective-permute-start | bytes 393224 | tf_op jit(solution)/shard_map/ppermute | solution.py:712
  (53 other events, 461.7 us)

commit v2 on v1

--- a/solution.py
+++ b/solution.py
@@ -425,76 +425,6 @@
     )(first_slot, q, k, v, inputs, wo, gain)
 
 
-def attn_bwd_kernel(
-    off_ref, q_ref, k_ref, v_ref, do_ref, mixed_ref, lse_ref,
-    dq_ref, dk_ref, dv_ref,
-):
-    h = pl.program_id(0)
-    seg = q_ref.shape[0] // 2
-    half = seg // 2
-    for stream in range(2):
-        base = stream * seg
-        lse_row = lse_ref[pl.ds(h, 1), base : base + seg]
-        weight = do_ref[base : base + seg].astype(F32) * mixed_ref[base : base + seg].astype(F32)
-        delta_row = jnp.sum(weight.T, axis=0, keepdims=True)
-        key_base = 2 * seg + stream * seg
-        pieces = []
-        if stream == 0:
-            pieces += [(start, half, 0, "mem") for start in range(0, 2 * seg, half)]
-        pieces += [(key_base, half, 0, "diag"), (key_base + half, half, half, "diag")]
-        dq_low = jnp.zeros((half, HEAD_DIM), F32)
-        dq_high = jnp.zeros((half, HEAD_DIM), F32)
-        for start, size, first, kind in pieces:
-            q = q_ref[base + first : base + seg]
-            do = do_ref[base + first : base + seg]
-            k = k_ref[start : start + size]
-            s = dot(k, q, NT) * EXP2_SCALE - lse_row[:, first:]
-            if kind == "mem":
-                slot = start + lax.broadcasted_iota(jnp.int32, s.shape, 0)
-                s = jnp.where(slot >= off_ref[0], s, masked_score)
-            else:
-                key = lax.broadcasted_iota(jnp.int32, s.shape, 0)
-                row = lax.broadcasted_iota(jnp.int32, s.shape, 1)
-                s = jnp.where(key <= row, s, masked_score)
-            p = jnp.exp2(s)
-            dp = dot(v_ref[start : start + size], do, NT)
-            ds = (p * (dp - delta_row[:, first:])).astype(BF16)
-            dv_ref[start : start + size] = dot(p.astype(BF16), do).astype(BF16)
-            dk_ref[start : start + size] = (dot(ds, q) * SCALE).astype(BF16)
-            dq = dot(ds, k, TN)
-            if first == 0:
-                dq_low = dq_low + dq[:half]
-                dq_high = dq_high + dq[half:]
-            else:
-                dq_high = dq_high + dq
-        dq_ref[base : base + half] = (dq_low * SCALE).astype(BF16)
-        dq_ref[base + half : base + seg] = (dq_high * SCALE).astype(BF16)
-
-
-def attn_bwd(first_slot, q, k, v, do, mixed, lse):
-    rows, width = q.shape
-    keys = k.shape[0]
-    q_spec = pl.BlockSpec((rows, HEAD_DIM), lambda h: (0, h))
-    k_spec = pl.BlockSpec((keys, HEAD_DIM), lambda h: (0, h))
-    return pl.pallas_call(
-        attn_bwd_kernel,
-        grid=(HEADS,),
-        out_shape=(
-            jax.ShapeDtypeStruct((rows, width), BF16),
-            jax.ShapeDtypeStruct((keys, width), BF16),
-            jax.ShapeDtypeStruct((keys, width), BF16),
-        ),
-        in_specs=[
-            pl.BlockSpec(memory_space=pltpu.SMEM),
-            q_spec, k_spec, k_spec, q_spec, q_spec, held(lse.shape),
-        ],
-        out_specs=(q_spec, k_spec, k_spec),
-        compiler_params=params(),
-        cost_estimate=cost(25e9, 24e6),
-        name="attn_bwd",
-    )(first_slot, q, k, v, do, mixed, lse)
-
-
 GELU_C = math.sqrt(2.0 / math.pi)
 GELU_A = 0.044715
 CHUNK = 512
@@ -707,6 +637,419 @@
     )(x, og, hidden, gain, wo, wh0, wh1, wr0, wr1)
 
 
+def attn_bwd_head(first_slot, q_ref, k_ref, v_ref, do_ref, mixed_ref, lse, dq_ref, dk_ref, dv_ref, cols):
+    seg = q_ref.shape[0] // 2
+    half = seg // 2
+    for stream in range(2):
+        base = stream * seg
+        rows = slice(base, base + seg)
+        lse_row = lse[:, rows]
+        weight = do_ref[rows, cols].astype(F32) * mixed_ref[rows, cols].astype(F32)
+        delta_row = jnp.sum(weight.T, axis=0, keepdims=True)
+        key_base = 2 * seg + stream * seg
+        pieces = []
+        if stream == 0:
+            pieces += [(start, half, 0, "mem") for start in range(0, 2 * seg, half)]
+        pieces += [(key_base, half, 0, "diag"), (key_base + half, half, half, "diag")]
+        dq_low = jnp.zeros((half, HEAD_DIM), F32)
+        dq_high = jnp.zeros((half, HEAD_DIM), F32)
+        for start, size, first, kind in pieces:
+            q = q_ref[base + first : base + seg, cols]
+            do = do_ref[base + first : base + seg, cols]
+            k = k_ref[start : start + size, cols]
+            s = dot(k, q, NT) * EXP2_SCALE - lse_row[:, first:]
+            if kind == "mem":
+                slot = start + lax.broadcasted_iota(jnp.int32, s.shape, 0)
+                s = jnp.where(slot >= first_slot, s, masked_score)
+            else:
+                key = lax.broadcasted_iota(jnp.int32, s.shape, 0)
+                row = lax.broadcasted_iota(jnp.int32, s.shape, 1)
+                s = jnp.where(key <= row, s, masked_score)
+            p = jnp.exp2(s)
+            dp = dot(v_ref[start : start + size, cols], do, NT)
+            ds = (p * (dp - delta_row[:, first:])).astype(BF16)
+            dv_ref[start : start + size, cols] = dot(p.astype(BF16), do).astype(BF16)
+            dk_ref[start : start + size, cols] = (dot(ds, q) * SCALE).astype(BF16)
+            dq = dot(ds, k, TN)
+            if first == 0:
+                dq_low = dq_low + dq[:half]
+                dq_high = dq_high + dq[half:]
+            else:
+                dq_high = dq_high + dq
+        dq_ref[base : base + half, cols] = (dq_low * SCALE).astype(BF16)
+        dq_ref[base + half : base + seg, cols] = (dq_high * SCALE).astype(BF16)
+
+
+class Chunk:
+    def __init__(self, data, left, order, landing, sems, place):
+        self.data, self.left, self.order = data, left, order
+        self.landing, self.sems = landing, sems
+        _, self.bit, self.across = place
+
+    def at(self, swap, away):
+        index = []
+        for b in self.left:
+            if b in self.order[:swap]:
+                index.append(self.bit(b))
+            elif swap < len(self.order) and b == self.order[swap]:
+                index.append(1 - self.bit(b) if away else self.bit(b))
+            else:
+                index.append(slice(None))
+        return tuple(index)
+
+    def copy(self, swap):
+        return remote(
+            self.data.at[self.at(swap, True)],
+            self.landing[swap],
+            (self.sems.at[0, swap], self.sems.at[1, swap]),
+            {"dp": self.across(self.order[swap])},
+        )
+
+    def start(self, swap):
+        self.copy(swap).start()
+
+    def settle(self, swap):
+        self.copy(swap).wait()
+        here = self.at(swap, False)
+        self.data[here] = add_low(self.data[here], self.landing[swap][...])
+
+    def last(self, swap):
+        self.copy(swap).wait()
+        return self.data[self.at(swap, False)].astype(F32) + self.landing[swap][...].astype(F32)
+
+
+def landings(left, order, block):
+    shapes, count = [], len(left)
+    for _ in order:
+        count -= 1
+        shapes.append(pltpu.VMEM((2,) * count + block, BF16))
+    return shapes
+
+
+BITS = (3, 2, 1, 0)
+ORDERS = ((0, 1, 2, 3), (1, 0, 2, 3))
+
+
+def attn_back_kernel(
+    off_ref, q_ref, k_ref, v_ref, do_ref, mix_ref, lse_ref, normed_ref, mixed_ref, ag_ref,
+    dq_ref, dk_ref, dv_ref, early_ref, late_ref,
+    core_out, core_in, own_ref, land_p, land_q, core_sems, chip_sems,
+):
+    step = pl.program_id(0)
+    last = pl.num_programs(0) - 1
+    place = mesh_place()
+    core = place[0]
+    partner = {"seq": 1 - core}
+    beside = ({"dp": place[2](0)}, {"dp": place[2](1)})
+    index = lax.div(step, 2)
+    rows = q_ref.shape[0]
+    keys = k_ref.shape[0]
+    pair = q_ref.shape[1]
+
+    @pl.when(step == 0)
+    def _():
+        greet((partner,) + beside)
+
+    def core_copy(which, index):
+        return remote(
+            core_out.at[which, index],
+            core_in.at[which, index],
+            (core_sems.at[0, which, index], core_sems.at[1, which, index]),
+            partner,
+        )
+
+    chunks = [
+        Chunk(own_ref.at[which], BITS, ORDERS[which][:1], [land], chip_sems.at[which], place)
+        for which, land in ((0, land_p), (1, land_q))
+    ]
+
+    head = 4 * jnp.where(lax.rem(step, 2) == 0, 1 - core, core) + 2 * index
+    for h in range(2):
+        attn_bwd_head(
+            off_ref[0], q_ref, k_ref, v_ref, do_ref, mix_ref, lse_ref[pl.ds(head + h, 1), :],
+            dq_ref, dk_ref, dv_ref, slice(h * HEAD_DIM, (h + 1) * HEAD_DIM),
+        )
+    grads = (
+        (
+            lambda: dot(normed_ref[keys - rows :], dq_ref[...], TN),
+            lambda: dot(normed_ref[...], dk_ref[...], TN),
+        ),
+        (
+            lambda: dot(normed_ref[...], dv_ref[...], TN),
+            lambda: dot(mixed_ref[...], ag_ref[...], TN),
+        ),
+    )
+
+    @pl.when(lax.rem(step, 2) == 0)
+    def _():
+        for which in range(2):
+            for side in range(2):
+                core_out[which, index, :, side * pair : (side + 1) * pair] = grads[which][side]().astype(BF16)
+            core_copy(which, index).start()
+
+    def own_grads(which, index, out_ref):
+        parts = [grads[which][side]() for side in range(2)]
+        core_copy(which, index).wait()
+        for side in range(2):
+            cols = slice(side * pair, (side + 1) * pair)
+            total = parts[side] + core_in[which, index, :, cols].astype(F32)
+            out_ref[:, :, :, :, :, cols] = total.astype(BF16).reshape(out_ref.shape[:5] + (pair,))
+
+    @pl.when(step == 1)
+    def _():
+        for which in range(2):
+            own_grads(which, 0, own_ref.at[which])
+            chunks[which].start(0)
+
+    @pl.when(step == last)
+    def _():
+        for which in range(2):
+            own_grads(which, 1, late_ref.at[which])
+        for which in range(2):
+            chunks[which].settle(0)
+            early_ref[which] = own_ref[(which,) + chunks[which].at(1, False)]
+
+
+def attn_back(first_slot, q, k, v, do, mixed, lse, normed, attn_grad):
+    rows, width = q.shape
+    keys = k.shape[0]
+    pair = 2 * HEAD_DIM
+    block = (width // 16, 2 * pair)
+
+    def by_pair(count):
+        def index(i):
+            core = lax.axis_index("seq")
+            half = jnp.where(lax.rem(i, 2) == 0, 1 - core, core)
+            return 0, 2 * half + lax.div(i, 2)
+
+        return pl.BlockSpec((count, pair), index)
+
+    early, late = (2, 2, 2, 2) + block, (2, 2, 2, 2, 2) + block
+    return pl.pallas_call(
+        attn_back_kernel,
+        grid=(4,),
+        out_shape=(
+            jax.ShapeDtypeStruct((rows, width), BF16),
+            jax.ShapeDtypeStruct((keys, width), BF16),
+            jax.ShapeDtypeStruct((keys, width), BF16),
+            jax.ShapeDtypeStruct(early, BF16),
+            jax.ShapeDtypeStruct(late, BF16),
+        ),
+        in_specs=[
+            pl.BlockSpec(memory_space=pltpu.SMEM),
+            by_pair(rows), by_pair(keys), by_pair(keys), by_pair(rows), by_pair(rows),
+            held(lse.shape), held(normed.shape), held(mixed.shape), by_pair(rows),
+        ],
+        out_specs=(by_pair(rows), by_pair(keys), by_pair(keys), held(early), held(late)),
+        scratch_shapes=[
+            pltpu.VMEM((2, 2, width, 2 * pair), BF16),
+            pltpu.VMEM((2, 2, width, 2 * pair), BF16),
+            pltpu.VMEM(late, BF16),
+            pltpu.VMEM(early[1:], BF16),
+            pltpu.VMEM(early[1:], BF16),
+            pltpu.SemaphoreType.DMA((2, 2, 2)),
+            pltpu.SemaphoreType.DMA((2, 2, 1)),
+        ],
+        compiler_params=pltpu.CompilerParams(
+            vmem_limit_bytes=VMEM_LIMIT, dimension_semantics=("arbitrary",),
+            collective_id=2, has_side_effects=True,
+        ),
+        cost_estimate=cost(45e9, 24e6),
+        name="attn_back",
+    )(first_slot, q, k, v, do, mixed, lse, normed, mixed, attn_grad)
+
+
+def rows_back_kernel(
+    dq_ref, dk_ref, dv_ref, raw_ref, ag_ref, gain_ref, gain_ffn_ref, wq_ref, wk_ref, wv_ref,
+    early_ref, late_ref, kept_h_ref, got_h_ref, kept_r_ref, got_r_ref,
+    mine_ref, theirs_ref, gains_ref, early_out_ref, late_out_ref, grad_h_ref, grad_r_ref,
+    rows_out, gain_acc, gain_in, ffn_ref, *scratch,
+):
+    step = pl.program_id(0)
+    last = pl.num_programs(0) - 1
+    place = mesh_place()
+    core, _, across = place
+    partner = {"seq": 1 - core}
+    lands, (row_sems, local_sems, gain_sems, chip_sems) = list(scratch[:-4]), scratch[-4:]
+
+    chunks = []
+
+    def chunk(data, left, order):
+        number = len(chunks)
+        mine = [lands.pop(0) for _ in order]
+        chunks.append(Chunk(data, left, order, mine, chip_sems.at[number], place))
+        return chunks[-1]
+
+    early, late, ffns = [], [], []
+    for which in range(2):
+        left = tuple(b for b in BITS if b != ORDERS[which][0])
+        early.append(chunk(early_ref.at[which], left, ORDERS[which][1:]))
+        late.append(chunk(late_ref.at[which], BITS, ORDERS[which]))
+        ffns.append(chunk(ffn_ref.at[which], (3, 2), (2, 3)))
+
+    def gain_copy(n):
+        device = partner if n == 0 else {"dp": across(n - 1)}
+        return remote(gain_acc.at[n], gain_in.at[n], (gain_sems.at[0, n], gain_sems.at[1, n]), device)
+
+    def row_copy(block):
+        stream = block // 2
+        return remote(
+            rows_out.at[block], theirs_ref.at[stream], (row_sems.at[0, stream], row_sems.at[1, stream]), partner
+        )
+
+    def row_keep(block):
+        stream = block // 2
+        return pltpu.make_async_copy(rows_out.at[block], mine_ref.at[stream], local_sems.at[stream])
+
+    @pl.when(step == 0)
+    def _():
+        greet((partner,) + tuple({"dp": across(b)} for b in range(4)))
+        for part in late + early:
+            part.start(0)
+        for which, (kept, got) in enumerate(((kept_h_ref, got_h_ref), (kept_r_ref, got_r_ref))):
+            ffn_ref[which] = add_low(kept[...], got[...]).reshape(ffn_ref.shape[1:])
+            ffns[which].start(0)
+        gain_acc[...] = jnp.zeros_like(gain_acc)
+
+    def normed_grad():
+        return dot(dk_ref[...], wk_ref[...], NT) + dot(dv_ref[...], wv_ref[...], NT)
+
+    unit, inverse = norm_parts(raw_ref[...].astype(F32))
+
+    @pl.when(step < 4)
+    def _():
+        gain_acc[0, 0:1] += jnp.sum(normed_grad() * unit, axis=0, keepdims=True)
+
+    @pl.when(step >= 4)
+    def _():
+        grad = normed_grad() + dot(dq_ref[...], wq_ref[...], NT)
+        gain_acc[0, 0:1] += jnp.sum(grad * unit, axis=0, keepdims=True)
+        rows_grad = norm_back(grad * gain_ref[...], unit, inverse)
+        rows_out[step - 4] = (rows_grad + ag_ref[...].astype(F32)).astype(BF16)
+
+    for block in range(4):
+        stays = core == block % 2
+        pl.when((step == block + 4) & stays)(row_keep(block).start)
+        pl.when((step == block + 4) & jnp.logical_not(stays))(row_copy(block).start)
+
+    @pl.when(step == 3)
+    def _():
+        for part in early:
+            part.settle(0)
+            part.start(1)
+
+    @pl.when(step == 6)
+    def _():
+        for part in late:
+            part.settle(0)
+            part.start(1)
+
+    @pl.when(step == last)
+    def _():
+        def gain_step(n):
+            gain_copy(n).wait()
+            total = gain_acc[n] + gain_in[n]
+            if n < 4:
+                gain_acc[n + 1] = total
+                gain_copy(n + 1).start()
+            else:
+                gains_ref[...] = total
+
+        gain_acc[0, 1:2] = gain_ffn_ref[...]
+        gain_copy(0).start()
+        for part in early:
+            part.settle(1)
+            part.start(2)
+        gain_step(0)
+        for part in ffns:
+            part.settle(0)
+            part.start(1)
+        gain_step(1)
+        for part in late:
+            part.settle(1)
+            part.start(2)
+        gain_step(2)
+        for which in range(2):
+            early_out_ref[which] = early[which].last(2)
+        gain_step(3)
+        for part in late:
+            part.settle(2)
+            part.start(3)
+        gain_step(4)
+        for which, out in enumerate((grad_h_ref, grad_r_ref)):
+            out[...] = ffns[which].last(1)
+        for which in range(2):
+            late_out_ref[which] = late[which].last(3)
+        for block in range(4):
+            stays = core == block % 2
+            pl.when(stays)(row_keep(block).wait)
+            pl.when(jnp.logical_not(stays))(row_copy(block).wait_send)
+        for stream in range(2):
+            row_copy(2 * stream).wait_recv()
+
+
+def rows_back(
+    dq, dk, dv, raw, attn_grad, gain, gain_ffn, wq, wk, wv, early, late, kept_h, got_h, kept_r, got_r
+):
+    keys, width = dk.shape
+    rows = dq.shape[0]
+    size = keys // 8
+    key_block = pl.BlockSpec((size, width), lambda i: (i, 0))
+    row_block = pl.BlockSpec((size, width), lambda i: (jnp.maximum(i - 4, 0), 0))
+    anywhere = pl.BlockSpec(memory_space=pl.ANY)
+    rows_shape = jax.ShapeDtypeStruct((2, size, width), BF16)
+    block = early.shape[-2:]
+    ffn_block = kept_h.shape[1:]
+    lands = []
+    for which in range(2):
+        lands += landings(BITS[1:], ORDERS[which][1:], block)
+        lands += landings(BITS, ORDERS[which], block)
+        lands += landings((3, 2), (2, 3), ffn_block)
+    out = (2,) + block
+    vector = (8, width)
+    return pl.pallas_call(
+        rows_back_kernel,
+        grid=(8,),
+        out_shape=(
+            rows_shape, rows_shape,
+            jax.ShapeDtypeStruct(vector, F32),
+            jax.ShapeDtypeStruct(out, F32),
+            jax.ShapeDtypeStruct(out, F32),
+            jax.ShapeDtypeStruct(ffn_block, F32),
+            jax.ShapeDtypeStruct(ffn_block, F32),
+        ),
+        in_specs=[
+            row_block, key_block, key_block, key_block, row_block,
+            held(gain.shape), held(gain_ffn.shape), held(wq.shape), held(wk.shape), held(wv.shape),
+            held(early.shape), held(late.shape),
+            held(kept_h.shape), held(got_h.shape), held(kept_r.shape), held(got_r.shape),
+        ],
+        out_specs=(
+            anywhere, anywhere, held(vector), held(out), held(out), held(ffn_block), held(ffn_block),
+        ),
+        scratch_shapes=[
+            pltpu.VMEM((4, size, width), BF16),
+            pltpu.VMEM((5,) + vector, F32),
+            pltpu.VMEM((5,) + vector, F32),
+            pltpu.VMEM((2, 2, 2) + ffn_block, BF16),
+        ] + lands + [
+            pltpu.SemaphoreType.DMA((2, 2)),
+            pltpu.SemaphoreType.DMA((2,)),
+            pltpu.SemaphoreType.DMA((2, 5)),
+            pltpu.SemaphoreType.DMA((6, 2, 4)),
+        ],
+        compiler_params=pltpu.CompilerParams(
+            vmem_limit_bytes=VMEM_LIMIT, dimension_semantics=("arbitrary",),
+            collective_id=3, has_side_effects=True,
+        ),
+        cost_estimate=cost(20e9, 24e6),
+        name="rows_back",
+    )(
+        dq, dk, dv, raw, attn_grad, gain, gain_ffn, wq, wk, wv,
+        early, late, kept_h, got_h, kept_r, got_r,
+    )
+
+
 def swap_dp(block, bit):
     count = lax.axis_size("dp")
     return lax.ppermute(block, "dp", [(i, i ^ (1 << bit)) for i in range(count)])
@@ -738,14 +1081,6 @@
     return own.astype(F32) + other.astype(F32)
 
 
-def reduce_gains(parts):
-    rank = lax.axis_index("dp")
-    parts = parts + swap_core(parts)
-    for bit in range(lax.axis_size("dp").bit_length() - 1):
-        parts = parts + swap_dp(parts, bit)
-    return lax.dynamic_index_in_dim(parts, rank, 0, False)
-
-
 def on_device_pair(
     inputs, memory, compressed, offsets, resets, w_query, w_key, w_value, w_output, w_hidden,
     w_return, w_compress, gain_attn, gain_ffn, out_grad, comp_grad,
@@ -837,33 +1172,24 @@
         ffn_in, og, hidden, gain_f, w_output, wh_other, w_hidden, wr_other, w_return
     )
     got_h, got_r = swap_dp(sent_h, 1), swap_dp(sent_r, 0)
-    dq, dk, dv = attn_bwd(first_slot, q, k, v, mixed_grad, mixed, lse)
-    grad_hidden = reduce_chips(kept_h, got_h, (2, 3), (3, 2))
-    grad_return = reduce_chips(kept_r, got_r, (2, 3), (3, 2)).T
-    output_part = dot(mixed, attn_grad, TN).astype(BF16)
-    query_part = dot(normed[2 * seg :], dq, TN).astype(BF16)
-    key_part = dot(normed, dk, TN).astype(BF16)
-    value_part = dot(normed, dv, TN).astype(BF16)
-    parts = [split_cores(part) for part in (query_part, key_part, value_part, output_part)]
-    own = jnp.concatenate([part[0] for part in parts], axis=1)
-    got_parts = swap_core(jnp.concatenate([part[1] for part in parts], axis=1))
-    grads = reduce_columns(own, got_parts)
-    cols = width // 2
-    grad_query, grad_key, grad_value, grad_output = (
-        grads[:, i * cols : (i + 1) * cols] for i in range(4)
-    )
-
-    normed_grad = dot(dk, w_key, NT) + dot(dv, w_value, NT)
-    query_back = dot(dq, w_query, NT)
-    normed_grad = normed_grad.at[2 * seg :].add(query_back)
-    gain_attn_grad = jnp.sum(normed_grad * normed_unit, axis=0)
-    input_unit, input_inverse = norm_parts(in_rows.astype(F32))
-    rows_grad = norm_back(normed_grad[2 * seg :] * gain_a, input_unit, input_inverse)
-    input_grad = (rows_grad + attn_grad.astype(F32)).astype(BF16)
-
-    gains = jnp.stack([gain_attn_grad, gain_ffn_grad.reshape(width)])
-    gains = gains.reshape(2, dp_count, width // dp_count).transpose(1, 0, 2)
-    gains = reduce_gains(gains)
+    dq, dk, dv, early, late = attn_back(
+        first_slot, q, k, v, mixed_grad, mixed, lse, normed, attn_grad
+    )
+    mine_rows, their_rows, gains, early_out, late_out, grad_hidden, grad_return = rows_back(
+        dq, dk, dv, all_rows, attn_grad, gain_a, gain_ffn_grad, w_query, w_key, w_value,
+        early, late, kept_h, got_h, kept_r, got_r,
+    )
+    grad_return = grad_return.T
+    pair = 2 * HEAD_DIM
+
+    def weight_grad(which, side):
+        cols = slice(side * pair, (side + 1) * pair)
+        return jnp.concatenate([early_out[which, :, cols], late_out[which, :, cols]], axis=1)
+
+    grad_query, grad_key = weight_grad(0, 0), weight_grad(0, 1)
+    grad_value, grad_output = weight_grad(1, 0), weight_grad(1, 1)
+    rank = lax.axis_index("dp")
+    gains = lax.dynamic_slice_in_dim(gains[:2], rank * (width // dp_count), width // dp_count, 1)
 
     def to_streams(a, b, which):
         swapped = lax.dynamic_index_in_dim(unused, which, 0, False)
@@ -891,7 +1217,7 @@
     return (
         place_rows(outputs),
         spread(comp_rows, swap_core(comp_rows)),
-        place_rows(input_grad),
+        spread(mine_rows, their_rows),
         grad_query,
         grad_key,
         grad_value,

time: 494 us -> 413 us (0.84)
  Pallas kernels: 147 us -> 250 us
  waiting for transfers between devices: 89.8 us -> 32.5 us
  matrix products: 83.4 us -> 26.9 us
  local copies, waits for them, and re-layouts: 76.6 us -> 47.3 us
  starting transfers between devices: 32.2 us -> 12.3 us
  other arithmetic: 52.3 us -> 32.7 us
    pallas_call x1 -> x2, Pallas kernels: 25.7 us -> 129 us  [the longest x1 76 us: rows_back(): pl.pallas_call(rows_back_kernel, grid=(8,), out_shape=(rows_shape, rows_s...]
    ppermute x26 -> x10, waiting for transfers between devices: 89.8 us -> 32.5 us  [swap_dp(): return lax.ppermute(block, 'dp', [(i, i ^ 1 << bit) for i in range(count)])]
    dot_general x12 -> x5, matrix products: 83.4 us -> 26.9 us  [dot(): return lax.dot_general(left, right, dims, preferred_element_type=F32)]
    ppermute x26 -> x10, starting transfers between devices: 29.6 us -> 10.7 us  [swap_dp(): return lax.ppermute(block, 'dp', [(i, i ^ 1 << bit) for i in range(count)])]
    dynamic_slice x5 -> x1, local copies, waits for them, and re-layouts: 12.9 us -> 2.81 us  [split_cores(): lax.dynamic_index_in_dim(cols, 1 - core, 1, False)]
    dynamic_slice x3 -> x1, local copies, waits for them, and re-layouts: 9.22 us -> 2.18 us  [split_cores(): lax.dynamic_index_in_dim(cols, core, 1, False)]
    unnamed x116 -> x72, local copies, waits for them, and re-layouts: 27.5 us -> 21.8 us
  transfers between devices with their start and end apart: 35 -> 16, of which waited for: 16 -> 8; matrix products, arithmetic and copies ran while one was open for 41% -> 21% of each run, Pallas kernels for 30% -> 61%
where the time goes in v2:
time: 413 us; the launch traced here: 408 us
  Pallas kernels  250 us (61%)
  local copies, waits for them, and re-layouts  47.3 us (11%)
  other arithmetic  32.7 us (8%)
  waiting for transfers between devices  32.5 us (8%)
  matrix products  26.9 us (7%)
  starting transfers between devices  12.3 us (3%)
  between operations  6.61 us (2%)
    pallas_call x1, Pallas kernels, ffn(): pl.pallas_call(ffn_kernel, grid=(steps,), out_shape=(low_rows, low_rows,...  90.2 us
    pallas_call x1, Pallas kernels, rows_back(): pl.pallas_call(rows_back_kernel, grid=(8,), out_shape=(rows_shape, rows_s...  76 us
    pallas_call x1, Pallas kernels, attn_back(): pl.pallas_call(attn_back_kernel, grid=(4,), out_shape=(jax.ShapeDtypeStru...  52.5 us
    ppermute x10, waiting for transfers between devices, swap_dp(): return lax.ppermute(block, 'dp', [(i, i ^ 1 << bit) for i in range(count)])  32.5 us
    pallas_call x1, Pallas kernels, attn_fwd(): pl.pallas_call(attn_fwd_kernel, grid=(4,), out_shape=(jax.ShapeDtypeStruc...  31.3 us
    dot_general x5, matrix products, dot(): return lax.dot_general(left, right, dims, preferred_element_type=F32)  26.9 us
    unnamed x72, local copies, waits for them, and re-layouts  21.8 us
    ppermute x10, starting transfers between devices, swap_dp(): return lax.ppermute(block, 'dp', [(i, i ^ 1 << bit) for i in range(count)])  10.7 us
  transfers between devices with their start and end apart: 16, of which 8 were waited for; matrix products, arithmetic and copies ran while one was open for 21% of the time, Pallas kernels for 61%

profile of v2, /device:TPU:0, one launch (start us, length us, event | category | flops | bytes accessed | tf_op | source)
XLA Modules:
  0.0 408.2 jit_solution(13859974601640477545)
XLA Ops:
  4.7 2.2 dynamic-slice_dynamic-update-slice_fusion.13
  6.9 2.4 dynamic-slice_dynamic-update-slice_fusion.12
  20.8 1.6 pad_maximum_fusion.3
  24.3 3.6 broadcast_select_fusion.1
  28.1 2.9 convert_reduce_fusion
  32.9 2.3 reshape.301
  35.3 5.9 %convolution_convert_fusion.3 = bf16[340,1024]{1,0:T(8,128)(2,1)S(1)} fusion(bf16[340,3072]{1,0:T(8,128)(2,1)} %reshape.301, bf16[3072,1024]{1,0:T(8,128)(2,1)} %param.27), kind=kOutput, calls=%fused_computation.37 | convolution fusion | flops 2139443200 | bytes 9076736 | tf_op jit(solution)/shard_map/dot_general | solution.py:317
  43.0 4.8 %convolution_convert_fusion = bf16[3072,1024]{0,1:T(8,128)(2,1)S(1)} fusion(bf16[340,3072]{1,0:T(8,128)(2,1)S(1)} %copy-done.11, bf16[340,1024]{1,0:T(8,128)(2,1)} %reshape.304), kind=kOutput, calls=%fused_computation.13 | convolution fusion | flops 2142240768 | bytes 9076736 | tf_op jit(solution)/shard_map/dot_general | solution.py:317
  47.8 2.2 constant_dynamic-slice_fusion.9
  50.0 2.8 copy.59
  53.3 3.2 fusion.1
  56.5 1.7 multiply_convert_fusion.normed_ref
  58.3 3.7 fusion.12.q_ref
  63.7 2.2 fusion.9
  65.9 3.2 copy.74
  69.1 2.0 fusion.44
  73.1 6.5 %convolution_convert_fusion.1.v_ref = bf16[2048,1024]{1,0:T(8,128)(2,1)} fusion(bf16[2048,1024]{1,0:T(8,128)(2,1)S(1)} %copy-done.10, bf16[1024,1024]{1,0:T(8,128)(2,1)S(1)} %copy-done.27), kind=kOutput, calls=%fused_computation.18 | convolution fusion | flops 4297064448 | bytes 10485760 | tf_op jit(solution)/shard_map/dot_general | solution.py:317
  79.5 6.0 %convolution_convert_fusion.2.k_ref = bf16[2048,1024]{1,0:T(8,128)(2,1)} fusion(bf16[2048,1024]{1,0:T(8,128)(2,1)S(1)} %copy-done.10, bf16[1024,1024]{1,0:T(8,128)(2,1)S(1)} %copy-done.26), kind=kOutput, calls=%fused_computation.19 | convolution fusion | flops 4297064448 | bytes 10485760 | tf_op jit(solution)/shard_map/dot_general | solution.py:317
  85.6 31.3 %attn_fwd.1 = (bf16[1024,1024]{1,0:T(8,128)(2,1)}, f32[1024,1024]{1,0:T(8,128)}, bf16[1024,1024]{1,0:T(8,128)(2,1)}, f32[8,1024]{1,0:T(8,128)}) custom-call(s32[1]{0:T(128)S(6)} %select_n.306.off_ref, bf16[1024,1024]{1,0:T(8,128)(2,1)} %fusion.12.q_ref, bf16[2048,1024]{1,0:T(8,128)(2,1)} %convolution_convert_fusion.2.k_ref, ...), custom_call_target="tpu_custom_call" | custom-call | flops 20000000000 | bytes 20000000 | tf_op jit(solution)/shard_map/attn_fwd/pallas_call | solution.py:408
  116.9 90.2 %ffn.1 = (bf16[1024,1024]{1,0:T(8,128)(2,1)}, bf16[1024,1024]{1,0:T(8,128)(2,1)}, bf16[1024,1024]{1,0:T(8,128)(2,1)}, f32[1,1024]{1,0:T(1,128)}, bf16[4,64,2048]...) custom-call(bf16[1024,1024]{1,0:T(8,128)(2,1)} %get-tuple-element.36., ...), custom_call_target="tpu_custom_call" | custom-call | flops 74999996416 | bytes 50000000 | tf_op jit(solution)/shard_map/ffn/pallas_call | solution.py:610
  210.6 52.5 %attn_back.1 = (bf16[1024,1024]{1,0:T(8,128)(2,1)}, bf16[2048,1024]{1,0:T(8,128)(2,1)}, bf16[2048,1024]{1,0:T(8,128)(2,1)}, bf16[2,2,2,2,64,512]{5,4,3,2,1,0:T(8,128)(2,1)}, bf16[2,2,2,2,2,64,512]{6,5,4,3,2,1,0:T(8,128)(2,1)}) custom-call(s32[1]{0:T(128)S(6)} %select_n.306.off_ref, bf16[1024,1024]{1,0:T(8,128)(2,1)} %fusion.12.q_ref, ...), custom_call_target="tpu_custom_call" | custom-call | flops 44999999488 | bytes 24000000 | tf_op jit(solution)/shard_map/attn_back/pallas_call | solution.py:828
  263.1 2.5 fusion.46
  268.2 2.2 copy.71
  271.4 76.0 %rows_back.1 = (bf16[2,256,1024]{2,1,0:T(8,128)(2,1)}, bf16[2,256,1024]{2,1,0:T(8,128)(2,1)}, f32[8,1024]{1,0:T(8,128)}, f32[2,64,512]{2,1,0:T(8,128)}, f32[2,64...) custom-call(bf16[1024,1024]{1,0:T(8,128)(2,1)} %get-tuple-element.43.dq_ref, ...), custom_call_target="tpu_custom_call" | custom-call | flops 20000000000 | bytes 24000000 | tf_op jit(solution)/shard_map/rows_back/pallas_call | solution.py:1010
  351.3 2.8 bitcast_select_fusion.3
  354.1 1.6 pad_maximum_fusion
  357.8 2.4 fusion.45
  363.5 15.6 %collective-permute-done.8 = bf16[2,2,2,192,256]{4,3,2,1,0:T(8,128)(2,1)S(1)} collective-permute-done((bf16[2,2,2,192,256]{4,3,2,1,0:T(8,128)(2,1)S(1)}, bf16[2,2,2,192,256]{4,3,2,1,0:T(8,128)(2,1)S(1)}, u32[]{:S(2)}, u32[]{:S(2)}) %collective-permute-start.8) | collective-permute-done | bytes 786464 | tf_op jit(solution)/shard_map/ppermute | solution.py:1055
  383.6 5.2 %collective-permute-done.9 = bf16[2,2,192,256]{3,2,1,0:T(8,128)(2,1)S(1)} collective-permute-done((bf16[2,2,192,256]{3,2,1,0:T(8,128)(2,1)S(1)}, bf16[2,2,192,256]{3,2,1,0:T(8,128)(2,1)S(1)}, u32[]{:S(2)}, u32[]{:S(2)}) %collective-permute-start.9) | collective-permute-done | bytes 393248 | tf_op jit(solution)/shard_map/ppermute | solution.py:1055
  391.8 4.6 %collective-permute-done.10 = bf16[2,192,256]{2,1,0:T(8,128)(2,1)S(1)} collective-permute-done((bf16[2,192,256]{2,1,0:T(8,128)(2,1)S(1)}, bf16[2,192,256]{2,1,0:T(8,128)(2,1)S(1)}, u32[]{:S(2)}, u32[]{:S(2)}) %collective-permute-start.10) | collective-permute-done | bytes 196640 | tf_op jit(solution)/shard_map/ppermute | solution.py:1055
  397.9 1.7 collective-permute-done.14
  402.6 2.9 collective-permute-done.15
  (143 shorter events, 50.7 us)
Async XLA Ops:
  0.6 8.7 %copy-start.13 = (bf16[4,256,1024]{2,1,0:T(8,128)(2,1)S(1)}, bf16[4,256,1024]{2,1,0:T(8,128)(2,1)}, u32[]{:S(2)}) copy-start(bf16[4,256,1024]{2,1,0:T(8,128)(2,1)} %param.16) | copy-start | bytes 6291460
  11.5 4.8 %copy-start.24 = (s32[4]{0:T(128)S(1)}, s32[4]{0:T(128)}, u32[]{:S(2)}) copy-start(s32[4]{0:T(128)} %param.20) | copy-start | bytes 52
  11.5 7.3 %copy-start.22 = (bf16[1024]{0:T(1024)(128)(2,1)S(1)}, bf16[1024]{0:T(1024)(128)(2,1)}, u32[]{:S(2)}) copy-start(bf16[1024]{0:T(1024)(128)(2,1)} %param.28) | copy-start | bytes 6148
  11.5 7.3 %copy-start.23 = (bf16[1024]{0:T(1024)(128)(2,1)S(1)}, bf16[1024]{0:T(1024)(128)(2,1)}, u32[]{:S(2)}) copy-start(bf16[1024]{0:T(1024)(128)(2,1)} %param.29) | copy-start | bytes 6148
  11.5 7.9 %copy-start.16 = (bf16[4,170,1024]{2,0,1:T(4,128)(2,1)S(1)}, bf16[4,170,1024]{2,0,1:T(4,128)(2,1)}, u32[]{:S(2)}) copy-start(bf16[4,170,1024]{2,0,1:T(4,128)(2,1)} %param.31) | copy-start | bytes 4177924
  14.7 9.7 %collective-permute-start = (bf16[7,256,1024]{2,1,0:T(8,128)(2,1)}, bf16[7,256,1024]{2,1,0:T(8,128)(2,1)}, u32[]{:S(2)}, u32[]{:S(2)}) collective-permute-start(bf16[7,256,1024]{2,1,0:T(8,128)(2,1)} %get-tuple-element.123), channel_id=1, source_target_pairs={{0,1},{1,0},{2,3},{3,2},{4,5},{5,4},{6,7},{7,6},{8,9},{9,8},{10,11... | collective-permute-start | bytes 11010056 | tf_op jit(solution)/shard_map/ppermute | solution.py:1059
  15.1 101.7 %collective-permute-start.1 = (bf16[1024,2048]{1,0:T(8,128)(2,1)}, bf16[1024,2048]{1,0:T(8,128)(2,1)}, u32[]{:S(2)}, u32[]{:S(2)}) collective-permute-start(bf16[1024,2048]{1,0:T(8,128)(2,1)} %wh1_ref.1), channel_id=1, source_target_pairs={{0,1},{1,0},{2,3},{3,2},{4,5},{5,4},{6,7},{7,6},{8,9},{9,8},{10,11... | collective-permute-start | bytes 12582920 | tf_op jit(solution)/shard_map/ppermute | solution.py:1059
  15.2 101.7 %collective-permute-start.2 = (bf16[2048,1024]{1,0:T(8,128)(2,1)}, bf16[2048,1024]{1,0:T(8,128)(2,1)}, u32[]{:S(2)}, u32[]{:S(2)}) collective-permute-start(bf16[2048,1024]{1,0:T(8,128)(2,1)} %wr1_ref.1), channel_id=1, source_target_pairs={{0,1},{1,0},{2,3},{3,2},{4,5},{5,4},{6,7},{7,6},{8,9},{9,8},{10,11... | collective-permute-start | bytes 12582920 | tf_op jit(solution)/shard_map/ppermute | solution.py:1059
  18.8 37.7 %copy-start.21 = (f32[1024]{0:T(1024)}, f32[1024]{0:T(1024)S(1)}, u32[]{:S(2)}) copy-start(f32[1024]{0:T(1024)S(1)} %convert_element_type.300) | copy-start | bytes 12292
  35.3 7.7 %copy-start.11 = (bf16[340,3072]{1,0:T(8,128)(2,1)S(1)}, bf16[340,3072]{1,0:T(8,128)(2,1)}, u32[]{:S(2)}) copy-start(bf16[340,3072]{1,0:T(8,128)(2,1)} %reshape.301) | copy-start | bytes 6266884
  41.2 6.6 %copy-start.5 = (bf16[340,1024]{1,0:T(8,128)(2,1)}, bf16[340,1024]{1,0:T(8,128)(2,1)S(1)}, u32[]{:S(2)}) copy-start(bf16[340,1024]{1,0:T(8,128)(2,1)S(1)} %convolution_convert_fusion.3) | copy-start | bytes 2088964
  42.9 220.2 %collective-permute-start.4 = (bf16[2,170,1024]{2,0,1:T(2,128)(2,1)}, bf16[2,170,1024]{2,0,1:T(2,128)(2,1)}, u32[]{:S(2)}, u32[]{:S(2)}) collective-permute-start(bf16[2,170,1024]{2,0,1:T(2,128)(2,1)} %copy.53), channel_id=1, source_target_pairs={{0,1},{1,0},{2,3},{3,2},{4,5},{5,4},{6,7},{7,6},{8,9},{9,8},{10,11... | collective-permute-start | bytes 2088968 | tf_op jit(solution)/shard_map/ppermute | solution.py:1059
  52.8 304.9 %collective-permute-start.7 = (bf16[3072,512]{1,0:T(8,128)(2,1)}, bf16[3072,512]{1,0:T(8,128)(2,1)}, u32[]{:S(2)}, u32[]{:S(2)}) collective-permute-start(bf16[3072,512]{1,0:T(8,128)(2,1)} %bitcast.164), channel_id=1, source_target_pairs={{0,1},{1,0},{2,3},{3,2},{4,5},{5,4},{6,7},{7,6},{8,9},{9,8},{10,11... | collective-permute-start | bytes 9437192 | tf_op jit(solution)/shard_map/ppermute | solution.py:1059
  58.3 5.4 %copy-start.3 = (bf16[7,256,1024]{2,1,0:T(8,128)(2,1)S(1)}, bf16[7,256,1024]{2,1,0:T(8,128)(2,1)}, u32[]{:S(2)}) copy-start(bf16[7,256,1024]{2,1,0:T(8,128)(2,1)} %copy-done.2) | copy-start | bytes 11010052
  73.1 6.5 %copy-start.26 = (bf16[1024,1024]{1,0:T(8,128)(2,1)S(1)}, bf16[1024,1024]{1,0:T(8,128)(2,1)}, u32[]{:S(2)}) copy-start(bf16[1024,1024]{1,0:T(8,128)(2,1)} %wk_ref.1) | copy-start | bytes 6291460
  208.4 142.9 %collective-permute-start.3 = (bf16[2,256,1024]{2,1,0:T(8,128)(2,1)S(1)}, bf16[2,256,1024]{2,1,0:T(8,128)(2,1)}, u32[]{:S(2)}, u32[]{:S(2)}) collective-permute-start(bf16[2,256,1024]{2,1,0:T(8,128)(2,1)S(1)} %dynamic-slice_bitcast_fusion), channel_id=1, source_target_pairs={{0,1},{1,0},{2,3},{3,2},{4,5},{5,4},{6,7},{7,6},{8,9},{9,8},{10,11... | collective-permute-start | bytes 3145736 | tf_op jit(solution)/shard_map/ppermute | solution.py:1059
  208.5 61.9 %collective-permute-start.5 = (bf16[4,64,2048]{2,1,0:T(8,128)(2,1)}, bf16[4,64,2048]{2,1,0:T(8,128)(2,1)S(1)}, u32[]{:S(2)}, u32[]{:S(2)}) collective-permute-start(bf16[4,64,2048]{2,1,0:T(8,128)(2,1)} %get-tuple-element.50), channel_id=1, source_target_pairs={{0,4},{2,6},{4,0},{6,2},{8,12},{10,14},{12,8},{14,10},{16,20},{18,... | collective-permute-start | bytes 3145736 | tf_op jit(solution)/shard_map/ppermute | solution.py:1055
  209.5 60.9 %collective-permute-start.6 = (bf16[4,64,2048]{2,1,0:T(8,128)(2,1)}, bf16[4,64,2048]{2,1,0:T(8,128)(2,1)}, u32[]{:S(2)}, u32[]{:S(2)}) collective-permute-start(bf16[4,64,2048]{2,1,0:T(8,128)(2,1)} %get-tuple-element.52), channel_id=1, source_target_pairs={{0,2},{2,0},{4,6},{6,4},{8,10},{10,8},{12,14},{14,12},{16,18},{18,... | collective-permute-start | bytes 3145736 | tf_op jit(solution)/shard_map/ppermute | solution.py:1055
  210.6 55.1 %copy-start.6 = (bf16[340,1024]{1,0:T(8,128)(2,1)S(1)}, bf16[340,1024]{1,0:T(8,128)(2,1)}, u32[]{:S(2)}) copy-start(bf16[340,1024]{1,0:T(8,128)(2,1)} %copy-done.5) | copy-start | bytes 2088964
  271.3 80.0 %copy-start.12 = (bf16[1024,1024]{1,0:T(8,128)(2,1)S(1)}, bf16[1024,1024]{1,0:T(8,128)(2,1)}, u32[]{:S(2)}) copy-start(bf16[1024,1024]{1,0:T(8,128)(2,1)} %get-tuple-element.38) | copy-start | bytes 6291460
  351.3 4.9 %copy-start.17 = (bf16[2,256,1024]{2,1,0:T(8,128)(2,1)S(1)}, bf16[2,256,1024]{2,1,0:T(8,128)(2,1)}, u32[]{:S(2)}) copy-start(bf16[2,256,1024]{2,1,0:T(8,128)(2,1)} %get-tuple-element.53) | copy-start | bytes 3145732
  351.3 4.9 %copy-start.18 = (bf16[2,256,1024]{2,1,0:T(8,128)(2,1)S(1)}, bf16[2,256,1024]{2,1,0:T(8,128)(2,1)}, u32[]{:S(2)}) copy-start(bf16[2,256,1024]{2,1,0:T(8,128)(2,1)} %get-tuple-element.54) | copy-start | bytes 3145732
  360.4 18.8 %collective-permute-start.8 = (bf16[2,2,2,192,256]{4,3,2,1,0:T(8,128)(2,1)S(1)}, bf16[2,2,2,192,256]{4,3,2,1,0:T(8,128)(2,1)S(1)}, u32[]{:S(2)}, u32[]{:S(2)}) collective-permute-start(bf16[2,2,2,192,256]{4,3,2,1,0:T(8,128)(2,1)S(1)} %fusion.16), channel_id=1, source_target_pairs={{0,2},{2,0},{4,6},{6,4},{8,10},{10,8},{12,14},{14,12},{16,18},{18,... | collective-permute-start | bytes 2359304 | tf_op jit(solution)/shard_map/ppermute | solution.py:1055
  361.8 18.6 %collective-permute-start.12 = (bf16[2,2,2,192,256]{4,3,0,2,1:T(8,128)(2,1)S(1)}, bf16[2,2,2,192,256]{4,3,0,2,1:T(8,128)(2,1)S(1)}, u32[]{:S(2)}, u32[]{:S(2)}) collective-permute-start(bf16[2,2,2,192,256]{4,3,0,2,1:T(8,128)(2,1)S(1)} %fusion.17), channel_id=1, source_target_pairs={{0,4},{2,6},{4,0},{6,2},{8,12},{10,14},{12,8},{14,10},{16,20},{18,... | collective-permute-start | bytes 2359304 | tf_op jit(solution)/shard_map/ppermute | solution.py:1055
  379.3 9.5 %collective-permute-start.9 = (bf16[2,2,192,256]{3,2,1,0:T(8,128)(2,1)S(1)}, bf16[2,2,192,256]{3,2,1,0:T(8,128)(2,1)S(1)}, u32[]{:S(2)}, u32[]{:S(2)}) collective-permute-start(bf16[2,2,192,256]{3,2,1,0:T(8,128)(2,1)S(1)} %fusion.22), channel_id=1, source_target_pairs={{0,4},{2,6},{4,0},{6,2},{8,12},{10,14},{12,8},{14,10},{16,20},{18,... | collective-permute-start | bytes 1179656 | tf_op jit(solution)/shard_map/ppermute | solution.py:1055
  380.6 9.2 %collective-permute-start.13 = (bf16[2,2,192,256]{3,2,1,0:T(8,128)(2,1)S(1)}, bf16[2,2,192,256]{3,2,1,0:T(8,128)(2,1)S(1)}, u32[]{:S(2)}, u32[]{:S(2)}) collective-permute-start(bf16[2,2,192,256]{3,2,1,0:T(8,128)(2,1)S(1)} %copy.69), channel_id=1, source_target_pairs={{0,2},{2,0},{4,6},{6,4},{8,10},{10,8},{12,14},{14,12},{16,18},{18,... | collective-permute-start | bytes 1179656 | tf_op jit(solution)/shard_map/ppermute | solution.py:1055
  383.5 22.9 %copy-start.20 = (f32[64,2048]{1,0:T(8,128)S(1)}, f32[64,2048]{1,0:T(8,128)}, u32[]{:S(2)}) copy-start(f32[64,2048]{1,0:T(8,128)} %get-tuple-element.195) | copy-start | bytes 1572868
  383.5 23.7 %copy-start.19 = (f32[64,2048]{1,0:T(8,128)S(1)}, f32[64,2048]{1,0:T(8,128)}, u32[]{:S(2)}) copy-start(f32[64,2048]{1,0:T(8,128)} %get-tuple-element.58) | copy-start | bytes 1572868
  388.9 7.5 %collective-permute-start.10 = (bf16[2,192,256]{2,1,0:T(8,128)(2,1)S(1)}, bf16[2,192,256]{2,1,0:T(8,128)(2,1)S(1)}, u32[]{:S(2)}, u32[]{:S(2)}) collective-permute-start(bf16[2,192,256]{2,1,0:T(8,128)(2,1)S(1)} %get-tuple-element.145), channel_id=1, source_target_pairs={{0,8},{2,10},{4,12},{6,14},{8,0},{10,2},{12,4},{14,6},{16,24},{18,... | collective-permute-start | bytes 589832 | tf_op jit(solution)/shard_map/ppermute | solution.py:1055
  390.0 9.7 %collective-permute-start.14 = (bf16[2,192,256]{2,1,0:T(8,128)(2,1)S(1)}, bf16[2,192,256]{2,1,0:T(8,128)(2,1)S(1)}, u32[]{:S(2)}, u32[]{:S(2)}) collective-permute-start(bf16[2,192,256]{2,1,0:T(8,128)(2,1)S(1)} %get-tuple-element.147), channel_id=1, source_target_pairs={{0,8},{2,10},{4,12},{6,14},{8,0},{10,2},{12,4},{14,6},{16,24},{18,... | collective-permute-start | bytes 589832 | tf_op jit(solution)/shard_map/ppermute | solution.py:1055
  396.5 6.1 %collective-permute-start.11 = (bf16[192,256]{1,0:T(8,128)(2,1)S(1)}, bf16[192,256]{1,0:T(8,128)(2,1)S(1)}, u32[]{:S(2)}, u32[]{:S(2)}) collective-permute-start(bf16[192,256]{1,0:T(8,128)(2,1)S(1)} %fusion.39), channel_id=1, source_target_pairs={{0,16},{2,18},{4,20},{6,22},{8,24},{10,26},{12,28},{14,30},{16,0},... | collective-permute-start | bytes 294920 | tf_op jit(solution)/shard_map/ppermute | solution.py:1055
  399.6 5.9 %collective-permute-start.15 = (bf16[192,256]{1,0:T(8,128)(2,1)S(1)}, bf16[192,256]{1,0:T(8,128)(2,1)S(1)}, u32[]{:S(2)}, u32[]{:S(2)}) collective-permute-start(bf16[192,256]{1,0:T(8,128)(2,1)S(1)} %fusion.41), channel_id=1, source_target_pairs={{0,16},{2,18},{4,20},{6,22},{8,24},{10,26},{12,28},{14,30},{16,0},... | collective-permute-start | bytes 294920 | tf_op jit(solution)/shard_map/ppermute | solution.py:1055
  (14 other events, 47.0 us)
